TPU v7x, 32 devices: a whole 2x2x4 slice. The times are simulated.
32 devices in a mesh: region: 8 (over z, x), pair: 4 (over y, core).
Axes of the slice: x: 2, y: 2, z: 4, core: 2. Of those that a mesh axis runs over, the one named last changes fastest.
Arguments:
- phi: bfloat16 [1024, 8, 32, 128], P('region', None, 'pair'), may hold values from -0.375 to 0.375
- potential: float32 [8, 32, 128], P('region', 'pair'), may hold values from -2 to 2
- pair_list: int32 [32, 2], replicated, may hold values from 0 to 7, as said below
- support: int32 [8, 8], replicated, may hold values 0 or 1
Outputs:
- intersection: float32 [32, 16384], P('pair', 'region')
- hamiltonian: float32 [32, 16384], P('pair', 'region')
- hphi: bfloat16 [1024, 8, 32, 128], P('region', None, 'pair')
Inputs may be any that keep to these rules, and one draw needn't show every extreme that they name: `pair_list`: each row is an ordered pair of block numbers; no pair appears twice.
All inputs are finite; a program needn't handle non-finite values.
Results may differ from a plain program's by a relative error of at most 0.0029.
Values may be sent and summed in bfloat16 or wider, within the bound.
A program may use at most 64 MiB of HBM per device.

v0:
```python
import jax
import jax.numpy as jnp
from jax import lax
from jax.sharding import PartitionSpec as P

W = 128


def padded_2(block, sides, width):
    for axis, dim in sides:
        count = lax.axis_size(axis)
        forward = [(i, i + 1) for i in range(count - 1)]
        forward.append((count - 1, 0))
        backward = [(target, source) for source, target in forward]
        low = lax.ppermute(
            lax.slice_in_dim(block, block.shape[dim] - width, None, axis=dim), axis, forward
        )
        high = lax.ppermute(lax.slice_in_dim(block, 0, width, axis=dim), axis, backward)
        block = jnp.concatenate([low, block, high], axis=dim)
    return block


def apply_region(padded, potential, keep_value):
    values = padded.astype(jnp.float32)
    center = values[:, 1:-1, 1:-1]
    laplace_sum = values[:, 2:, 1:-1] + values[:, :-2, 1:-1] - 6.0 * center
    laplace_sum = laplace_sum + values[:, 1:-1, 2:] + values[:, 1:-1, :-2]
    z_padded = jnp.pad(center, ((0, 0), (0, 0), (0, 0), (1, 1)))
    laplace_sum = laplace_sum + z_padded[..., 2:] + z_padded[..., :-2]
    applied = (-0.5 * laplace_sum + potential[None] * center) * keep_value
    return applied.astype(jnp.bfloat16)


def local(phi, potential, pair_list, support):
    region_id = lax.axis_index("region")
    block_count = support.shape[0]
    all_funcs = block_count * W
    row_count = phi.shape[2]
    depth = phi.shape[3]
    plane_count = potential.shape[0]
    block_flags = lax.dynamic_slice_in_dim(support, region_id, 1, 1)[:, 0]
    func_live = jnp.repeat(block_flags > 0, W)
    region_data = lax.all_to_all(phi, "region", split_axis=1, concat_axis=0, tiled=True)
    confined = jnp.where(func_live[:, None, None, None], region_data, jnp.zeros_like(region_data))
    padded = padded_2(confined, (("region", 1), ("pair", 2)), 1)
    keep_values = block_flags.astype(jnp.float32)
    stacked = padded.reshape(block_count, W, plane_count + 2, row_count + 2, depth)
    applied_region = lax.map(
        lambda members: apply_region(members[0], potential, members[1]), (stacked, keep_values)
    )
    applied_region = applied_region.reshape(all_funcs, plane_count, row_count, depth)
    cell_count = plane_count * row_count * depth
    flat_data = confined.reshape(all_funcs, cell_count)
    flat_applied = applied_region.reshape(all_funcs, cell_count)
    contract_dims = (((1,), (1,)), ((), ()))

    def pair_terms(pair_row):
        left_rows = lax.dynamic_slice_in_dim(flat_data, pair_row[0] * W, W, 0)
        right_rows = lax.dynamic_slice_in_dim(flat_data, pair_row[1] * W, W, 0)
        ham_rows = lax.dynamic_slice_in_dim(flat_applied, pair_row[1] * W, W, 0)
        return (
            lax.dot_general(
                left_rows, right_rows, contract_dims, preferred_element_type=jnp.float32
            ),
            lax.dot_general(left_rows, ham_rows, contract_dims, preferred_element_type=jnp.float32),
        )

    intersection_part, hamil_part = lax.map(pair_terms, pair_list)
    pair_count = pair_list.shape[0]
    intersection_part = intersection_part.reshape(pair_count, W * W)
    hamil_part = hamil_part.reshape(pair_count, W * W)
    intersection_cols, hamil_cols = (
        lax.psum_scatter(intersection_part, "region", scatter_dimension=1, tiled=True),
        lax.psum_scatter(hamil_part, "region", scatter_dimension=1, tiled=True),
    )
    intersection, hamiltonian = (
        lax.psum_scatter(intersection_cols, "pair", scatter_dimension=0, tiled=True),
        lax.psum_scatter(hamil_cols, "pair", scatter_dimension=0, tiled=True),
    )
    hphi_out = lax.all_to_all(applied_region, "region", split_axis=0, concat_axis=1, tiled=True)
    return (intersection, hamiltonian, hphi_out)


def solution(mesh):
    in_specs = (P("region", None, "pair", None), P("region", "pair", None), P(), P())
    out_specs = (P("pair", "region"), P("pair", "region"), P("region", None, "pair", None))
    return jax.shard_map(local, mesh=mesh, in_specs=in_specs, out_specs=out_specs, check_vma=False)
```

profile of v0, /device:TPU:0, one launch (start us, length us, event | category | flops | bytes accessed | tf_op | source)
XLA Modules:
  0.0 635.3 jit_solution(6267926977608659590)
XLA Ops:
  7.2 3.3 copy.12
  10.5 7.4 %all-to-all-start = ((bf16[128,8,8,128]{3,2,0,1:T(8,128)(2,1)}), bf16[128,8,8,128]{3,2,0,1:T(8,128)(2,1)S(1)}, u32[]{:S(2)}, u32[]{:S(2)}) async-start(bf16[128,8,8,128]{3,2,0,1:T(8,128)(2,1)} %copy.12), calls=%async_computation | async-start | bytes 4194304 | tf_op jit(solution)/shard_map/all_to_all | solution.py:43
  18.2 47.9 %all-to-all-done = bf16[128,8,8,128]{3,2,0,1:T(8,128)(2,1)S(1)} async-done(((bf16[128,8,8,128]{3,2,0,1:T(8,128)(2,1)}), bf16[128,8,8,128]{3,2,0,1:T(8,128)(2,1)S(1)}, u32[]{:S(2)}, u32[]{:S(2)}) %all-to-all-start) | async-done | bytes 2097184 | tf_op jit(solution)/shard_map/all_to_all | solution.py:43
  66.1 3.7 bitcast_select_fusion.1
  71.3 3.3 collective-permute-start.1
  74.6 85.8 %collective-permute-done = bf16[1024,1,8,128]{3,2,0,1:T(8,128)(2,1)S(1)} collective-permute-done((bf16[1024,1,8,128]{3,2,0,1:T(8,128)(2,1)S(1)}, bf16[1024,1,8,128]{3,2,0,1:T(8,128)(2,1)S(1)}, u32[]{:S(2)}, u32[]{:S(2)}) %collective-permute-start) | collective-permute-done | bytes 2097184 | tf_op jit(solution)/shard_map/ppermute | solution.py:15
  160.4 2.2 collective-permute-done.1
  162.6 2.6 pad_maximum_fusion.3
  170.1 12.2 %collective-permute-done.2 = bf16[1024,3,1,128]{3,0,2,1:T(8,128)(2,1)} collective-permute-done((bf16[1024,3,1,128]{3,0,2,1:T(8,128)(2,1)S(1)}, bf16[1024,3,1,128]{3,0,2,1:T(8,128)(2,1)}, u32[]{:S(2)}, u32[]{:S(2)}) %collective-permute-start.2) | collective-permute-done | bytes 786464 | tf_op jit(solution)/shard_map/ppermute | solution.py:15
  182.3 2.3 copy.15
  184.6 2.4 copy.16
  187.0 10.7 %pad_maximum_fusion = bf16[1024,3,10,128]{3,2,0,1:T(8,128)(2,1)} fusion(bf16[1024,3,1,128]{3,2,0,1:T(2,128)(2,1)S(1)} %copy.16, bf16[1024,1,8,128]{3,2,0,1:T(8,128)(2,1)S(1)} %copy-done.7, bf16[1024,1,8,128]{3,2,0,1:T(8,128)(2,1)S(1)} %copy-done.1, bf16[1024,1,8,128]{3,2,0,1:T(8,128)(2,1)S(1)} %copy-done.5, bf16[1024,3,1,128]{3,2,0,1:T(2,128)(2,1)S(1)} %copy.15), kind=kLoop, calls=%fused_computation.25 | loop fusion | flops 39321600 | bytes 15728640 | tf_op jit(solution)/shard_map/concatenate | solution.py:19
  197.7 26.9 %while.24 = (s32[]{:T(128)}, bf16[8,128,1,8,128]{4,3,2,1,0:T(8,128)(2,1)S(1)}, bf16[8,128,3,10,128]{4,3,1,0,2:T(8,128)(2,1)}, f32[1,8,128]{2,1,0:T(8,128)S(1)}, f32[8]{0:T(128)S(1)}, /*index=5*/s32[]{:T(128)}) while((s32[]{:T(128)}, bf16[8,128,1,8,128]{4,3,2,1,0:T(8,128)(2,1)S(1)}, bf16[8,128,3,10,128]{4,3,1,0,2:T(8,128)(2,1)}, ...), condition=%wide.region_1.2_spmd, body=%wide.region_0.1_spmd.sunk | while | flops 2064386 | bytes 6885469 | solution.py:48
  224.6 1.9 copy.33
  226.5 181.9 %while.25 = (s32[]{:T(128)}, f32[32,128,128]{2,1,0:T(8,128)}, f32[32,128,128]{2,1,0:T(8,128)}, s32[32,2]{0,1:T(2,128)S(1)}, bf16[1024,1024]{1,0:T(8,128)(2,1)}, ...) while((s32[]{:T(128)}, f32[32,128,128]{2,1,0:T(8,128)}, ...), condition=%wide.region_3.4_spmd, body=%wide.region_2.3_spmd.sunk | while | flops 67108872 | bytes 1180917 | solution.py:68
  239.8 1.9 fusion.29
  251.2 1.9 fusion.29
  273.9 1.9 fusion.29
  279.6 1.9 fusion.29
  291.0 1.9 fusion.29
  325.1 1.9 fusion.29
  370.5 1.9 fusion.29
  376.2 1.9 fusion.29
  393.2 1.9 fusion.29
  408.4 4.1 copy.31
  414.1 2.5 copy.32
  416.7 3.7 all-to-all-start.1
  420.4 91.8 %reduce-scatter.9.cloned.1.call-done = f32[32,2048]{1,0:T(8,128)} async-done(((f32[32,16384]{1,0:T(8,128)}), f32[32,2048]{1,0:T(8,128)}) %reduce-scatter.9.cloned.1.call-update) | async-done | bytes 262160 | tf_op jit(solution)/shard_map/reduce_scatter | solution.py:74
  512.3 71.3 %reduce-scatter.5.cloned.1.call-done = f32[32,2048]{1,0:T(8,128)} async-done(((f32[32,16384]{1,0:T(8,128)}), f32[32,2048]{1,0:T(8,128)}) %reduce-scatter.5.cloned.1.call-update) | async-done | bytes 262160 | tf_op jit(solution)/shard_map/reduce_scatter | solution.py:73
  583.6 1.9 copy.19
  585.5 20.2 %reduce-scatter.11.cloned.1.call-done = f32[8,2048]{1,0:T(8,128)} async-done(((f32[32,2048]{1,0:T(8,128)}), f32[8,2048]{1,0:T(8,128)}) %reduce-scatter.11.cloned.1.call-update) | async-done | bytes 65552 | tf_op jit(solution)/shard_map/reduce_scatter | solution.py:78
  605.7 23.1 %reduce-scatter.7.cloned.1.call-done = f32[8,2048]{1,0:T(8,128)} async-done(((f32[32,2048]{1,0:T(8,128)}), f32[8,2048]{1,0:T(8,128)}) %reduce-scatter.7.cloned.1.call-update) | async-done | bytes 65552 | tf_op jit(solution)/shard_map/reduce_scatter | solution.py:77
  (197 shorter events, 158.4 us)
Async XLA Ops:
  10.5 7.4 %copy-start.11 = (s32[8,8]{1,0:T(8,128)S(1)}, s32[8,8]{1,0:T(8,128)}, u32[]{:S(2)}) copy-start(s32[8,8]{1,0:T(8,128)} %param.11) | copy-start | bytes 772
  10.5 55.6 %all-to-all-start = ((bf16[128,8,8,128]{3,2,0,1:T(8,128)(2,1)}), bf16[128,8,8,128]{3,2,0,1:T(8,128)(2,1)S(1)}, u32[]{:S(2)}, u32[]{:S(2)}) async-start(bf16[128,8,8,128]{3,2,0,1:T(8,128)(2,1)} %copy.12), calls=%async_computation | async-start | bytes 4194304 | tf_op jit(solution)/shard_map/all_to_all | solution.py:43
  17.8 494.4 %reduce-scatter.9.cloned.1.call-start = ((), (), s32[]{:S(2)}) async-start(), calls=%async_computation.8 | async-start | bytes 2359296 | tf_op jit(solution)/shard_map/reduce_scatter | solution.py:74
  69.8 95.4 %copy-start = (bf16[1024,1,8,128]{3,2,0,1:T(8,128)(2,1)}, bf16[1024,1,8,128]{3,2,0,1:T(8,128)(2,1)S(1)}, u32[]{:S(2)}) copy-start(bf16[1024,1,8,128]{3,2,0,1:T(8,128)(2,1)S(1)} %bitcast_select_fusion.1) | copy-start | bytes 6291460
  69.8 90.6 %collective-permute-start = (bf16[1024,1,8,128]{3,2,0,1:T(8,128)(2,1)S(1)}, bf16[1024,1,8,128]{3,2,0,1:T(8,128)(2,1)S(1)}, u32[]{:S(2)}, u32[]{:S(2)}) collective-permute-start(bf16[1024,1,8,128]{3,2,0,1:T(8,128)(2,1)S(1)} %bitcast_select_fusion.1), channel_id=1, source_target_pairs={{0,4},{4,8},{8,12},{12,16},{16,20},{20,24},{24,28},{28,0},{1,5},{5... | collective-permute-start | bytes 6291464 | tf_op jit(solution)/shard_map/ppermute | solution.py:15
  71.3 91.3 %collective-permute-start.1 = (bf16[1024,1,8,128]{3,2,0,1:T(8,128)(2,1)S(1)}, bf16[1024,1,8,128]{3,2,0,1:T(8,128)(2,1)S(1)}, u32[]{:S(2)}, u32[]{:S(2)}) collective-permute-start(bf16[1024,1,8,128]{3,2,0,1:T(8,128)(2,1)S(1)} %bitcast_select_fusion.1), channel_id=1, source_target_pairs={{4,0},{8,4},{12,8},{16,12},{20,16},{24,20},{28,24},{0,28},{5,1},{9... | collective-permute-start | bytes 6291464 | tf_op jit(solution)/shard_map/ppermute | solution.py:18
  160.4 4.8 copy-start.4
  162.6 2.7 copy-start.6
  165.4 16.9 %collective-permute-start.2 = (bf16[1024,3,1,128]{3,0,2,1:T(8,128)(2,1)S(1)}, bf16[1024,3,1,128]{3,0,2,1:T(8,128)(2,1)}, u32[]{:S(2)}, u32[]{:S(2)}) collective-permute-start(bf16[1024,3,1,128]{3,0,2,1:T(8,128)(2,1)S(1)} %copy.13), channel_id=1, source_target_pairs={{0,1},{1,2},{2,3},{3,0},{4,5},{5,6},{6,7},{7,4},{8,9},{9,10},{10,1... | collective-permute-start | bytes 2359304 | tf_op jit(solution)/shard_map/ppermute | solution.py:15
  166.4 18.2 %collective-permute-start.3 = (bf16[1024,3,1,128]{3,0,2,1:T(8,128)(2,1)}, bf16[1024,3,1,128]{3,0,2,1:T(8,128)(2,1)}, u32[]{:S(2)}, u32[]{:S(2)}) collective-permute-start(bf16[1024,3,1,128]{3,0,2,1:T(8,128)(2,1)} %copy.14), channel_id=1, source_target_pairs={{1,0},{2,1},{3,2},{0,3},{5,4},{6,5},{7,6},{4,7},{9,8},{10,9},{11,1... | collective-permute-start | bytes 2359304 | tf_op jit(solution)/shard_map/ppermute | solution.py:18
  168.4 18.6 %copy-start.7 = (bf16[1024,1,8,128]{3,2,0,1:T(8,128)(2,1)S(1)}, bf16[1024,1,8,128]{3,2,0,1:T(8,128)(2,1)}, u32[]{:S(2)}) copy-start(bf16[1024,1,8,128]{3,2,0,1:T(8,128)(2,1)} %copy-done.6) | copy-start | bytes 6291460
  170.1 16.9 %copy-start.1 = (bf16[1024,1,8,128]{3,2,0,1:T(8,128)(2,1)S(1)}, bf16[1024,1,8,128]{3,2,0,1:T(8,128)(2,1)}, u32[]{:S(2)}) copy-start(bf16[1024,1,8,128]{3,2,0,1:T(8,128)(2,1)} %copy-done) | copy-start | bytes 6291460
  170.1 16.9 %copy-start.5 = (bf16[1024,1,8,128]{3,2,0,1:T(8,128)(2,1)S(1)}, bf16[1024,1,8,128]{3,2,0,1:T(8,128)(2,1)}, u32[]{:S(2)}) copy-start(bf16[1024,1,8,128]{3,2,0,1:T(8,128)(2,1)} %copy-done.4) | copy-start | bytes 6291460
  187.0 10.7 %copy-start.2 = (bf16[8,128,1,8,128]{4,3,2,1,0:T(8,128)(2,1)S(1)}, bf16[8,128,1,8,128]{4,3,2,1,0:T(8,128)(2,1)}, u32[]{:S(2)}) copy-start(bf16[8,128,1,8,128]{4,3,2,1,0:T(8,128)(2,1)} %custom-call) | copy-start | bytes 6291460
  187.0 10.7 %copy-start.9 = (f32[1,8,128]{2,1,0:T(8,128)S(1)}, f32[1,8,128]{2,1,0:T(8,128)}, u32[]{:S(2)}) copy-start(f32[1,8,128]{2,1,0:T(8,128)} %param.9) | copy-start | bytes 12292
  224.6 2.0 copy-start.3
  224.6 2.0 copy-start.10
  412.5 1.6 copy-start.8
  412.5 171.0 %reduce-scatter.5.cloned.1.call-start = ((), (), s32[]{:S(2)}) async-start(), calls=%async_computation.6 | async-start | bytes 2359296 | tf_op jit(solution)/shard_map/reduce_scatter | solution.py:73
  416.7 166.9 %all-to-all-start.1 = ((bf16[1024,1,8,128]{3,2,1,0:T(8,128)(2,1)}), bf16[1024,1,8,128]{3,2,1,0:T(8,128)(2,1)S(1)}, u32[]{:S(2)}, u32[]{:S(2)}) async-start(bf16[1024,1,8,128]{3,2,1,0:T(8,128)(2,1)} %bitcast.74), calls=%async_computation.5 | async-start | bytes 4194304 | tf_op jit(solution)/shard_map/all_to_all | solution.py:80
  420.4 185.3 %reduce-scatter.11.cloned.1.call-start = ((), (), s32[]{:S(2)}) async-start(), calls=%async_computation.9 | async-start | bytes 327680 | tf_op jit(solution)/shard_map/reduce_scatter | solution.py:78
  512.2 116.5 %reduce-scatter.7.cloned.1.call-start = ((), (), s32[]{:S(2)}) async-start(), calls=%async_computation.7 | async-start | bytes 327680 | tf_op jit(solution)/shard_map/reduce_scatter | solution.py:77
Sparse Core Ops, SparseCore 0:
  412.7 99.5 reduce-scatter.8
  516.3 67.1 reduce-scatter.4
  586.6 19.0 reduce-scatter.10
  608.7 20.0 reduce-scatter.6
where the time goes:
time: 638 us; the launch traced here: 635 us
  waiting for transfers between devices  354 us (55%)
  matrix products  121 us (19%)
  local copies, waits for them, and re-layouts  45.5 us (7%)
  loops' own time  41.5 us (7%)
  other arithmetic  40.8 us (6%)
  starting transfers between devices  17.8 us (3%)
  between operations  14 us (2%)
    ppermute x2, waiting for transfers between devices, padded_2(): lax.ppermute(lax.slice_in_dim(block, block.shape[dim] - width, None, axis...  98 us
    reduce_scatter x1, waiting for transfers between devices, local(): lax.psum_scatter(hamil_part, 'region', scatter_dimension=1, tiled=True)  91.8 us
    reduce_scatter x1, waiting for transfers between devices, local(): lax.psum_scatter(intersection_part, 'region', scatter_dimension=1, tiled=...  71.3 us
    dot_general x32, matrix products, pair_terms(): lax.dot_general(left_rows, ham_rows, contract_dims, preferred_element_typ...  60.7 us
    dot_general x32, matrix products, pair_terms(): lax.dot_general(left_rows, right_rows, contract_dims, preferred_element_t...  60.5 us
    all_to_all x1, waiting for transfers between devices, local(): lax.all_to_all(phi, 'region', split_axis=1, concat_axis=0, tiled=True)  47.9 us
    another operation x1, loops' own time, local(): intersection_part, hamil_part = lax.map(pair_terms, pair_list)  41.2 us
    reduce_scatter x1, waiting for transfers between devices, local(): lax.psum_scatter(intersection_cols, 'pair', scatter_dimension=0, tiled=True)  23.1 us
  transfers between devices with their start and end apart: 10, of which 8 were waited for; matrix products, arithmetic and copies ran while one was open for 2% of the time, Pallas kernels for 0%

commit v1 on v0

v1 whole, which is shorter than its diff:
```python
import jax
import jax.numpy as jnp
from jax import lax
from jax.experimental import pallas as pl
from jax.experimental.pallas import tpu as pltpu
from jax.sharding import PartitionSpec as P

W = 128


def pair_kernel(pairs_ref, data_ref, applied_ref, out_ref):
    contract = (((1,), (1,)), ((), ()))

    def step(k, carry):
        left = data_ref[pl.ds(pl.multiple_of(pairs_ref[k, 0] * W, W), W), :]
        rows = pl.ds(pl.multiple_of(pairs_ref[k, 1] * W, W), W)
        right = jnp.concatenate([data_ref[rows, :], applied_ref[rows, :]], axis=0)
        both = lax.dot_general(left, right, contract, preferred_element_type=jnp.float32)
        out_ref[k, 0] = both[:, :W]
        out_ref[k, 1] = both[:, W:]
        return carry

    lax.fori_loop(0, pairs_ref.shape[0], step, 0)


def pair_blocks(pair_list, data, applied):
    count = pair_list.shape[0]
    return pl.pallas_call(
        pair_kernel,
        out_shape=jax.ShapeDtypeStruct((count, 2, W, W), jnp.float32),
        in_specs=[
            pl.BlockSpec(memory_space=pltpu.SMEM),
            pl.BlockSpec(memory_space=pltpu.VMEM),
            pl.BlockSpec(memory_space=pltpu.VMEM),
        ],
        out_specs=pl.BlockSpec(memory_space=pltpu.VMEM),
        compiler_params=pltpu.CompilerParams(vmem_limit_bytes=32 * 2**20),
        cost_estimate=pl.CostEstimate(
            flops=count * 4 * W * W * data.shape[1],
            bytes_accessed=data.size * 4 + count * 8 * W * W,
            transcendentals=0,
        ),
    )(pair_list, data, applied)


def local(phi, potential, pair_list, support):
    region_id = lax.axis_index("region")
    region_count = lax.axis_size("region")
    pair_axis = lax.axis_size("pair")
    func_count, _, row_count, depth = phi.shape
    owners = (region_id * func_count + jnp.arange(func_count)) // W
    live = support[owners]
    confined = jnp.where((live > 0)[:, :, None, None], phi, jnp.zeros_like(phi))
    forward = [(i, (i + 1) % pair_axis) for i in range(pair_axis)]
    backward = [(target, source) for source, target in forward]
    low = lax.ppermute(confined[:, :, -1:], "pair", forward)
    high = lax.ppermute(confined[:, :, :1], "pair", backward)
    grid_potential = lax.all_gather(potential, "region", axis=0, tiled=True)
    data = lax.all_to_all(confined, "region", split_axis=1, concat_axis=0, tiled=True)

    center = confined.astype(jnp.float32)
    total = jnp.roll(center, -1, axis=1) + jnp.roll(center, 1, axis=1) - 6.0 * center
    below = jnp.concatenate([low.astype(jnp.float32), center[:, :, :-1]], axis=2)
    above = jnp.concatenate([center[:, :, 1:], high.astype(jnp.float32)], axis=2)
    total = total + above + below
    z_padded = jnp.pad(center, ((0, 0), (0, 0), (0, 0), (1, 1)))
    total = total + z_padded[..., 2:] + z_padded[..., :-2]
    keep = live.astype(jnp.float32)[:, :, None, None]
    applied = ((-0.5 * total + grid_potential[None] * center) * keep).astype(jnp.bfloat16)
    applied_data = lax.all_to_all(applied, "region", split_axis=1, concat_axis=0, tiled=True)

    flat = (func_count * region_count, -1)
    blocks = pair_blocks(pair_list, data.reshape(flat), applied_data.reshape(flat))
    listed = pair_list.shape[0] // pair_axis
    width = W // region_count
    parts = blocks.reshape(pair_axis, listed, 2, W, W)
    parts = lax.all_to_all(parts, "pair", split_axis=0, concat_axis=0, tiled=True)
    sums = jnp.sum(parts, axis=0)
    sums = sums.reshape(listed, 2, region_count, width, W).transpose(2, 1, 0, 3, 4)
    sums = lax.all_to_all(sums, "region", split_axis=0, concat_axis=0, tiled=True)
    result = jnp.sum(sums, axis=0).reshape(2, listed, width * W)
    return result[0], result[1], applied


def solution(mesh):
    in_specs = (P("region", None, "pair", None), P("region", "pair", None), P(), P())
    out_specs = (P("pair", "region"), P("pair", "region"), P("region", None, "pair", None))
    return jax.shard_map(local, mesh=mesh, in_specs=in_specs, out_specs=out_specs, check_vma=False)
```

time: 638 us -> 238 us (0.37)
  waiting for transfers between devices: 354 us -> 63.2 us
  matrix products: 121 us -> 0 us
  blocking collectives: 0 us -> 109 us
  loops' own time: 41.5 us -> 0 us
  other arithmetic: 40.8 us -> 14.5 us
  local copies, waits for them, and re-layouts: 45.5 us -> 23.1 us
  between operations: 14 us -> 0.83 us
  Pallas kernels: 0 us -> 10.6 us
    reduce_scatter x4 -> x0, waiting for transfers between devices: 206 us -> none  [the longest x1 91.8 us: local(): lax.psum_scatter(hamil_part, 'region', scatter_dimension=1, tiled=True)]
    dot_general x64 -> x0, matrix products: 121 us -> none  [the longest x32 60.7 us: pair_terms(): lax.dot_general(left_rows, ham_rows, contract_dims, preferred_element_typ...]
    ppermute x4 -> x2, waiting for transfers between devices: 100 us -> 0.01 us  [the longest x1 0.01 us: local(): high = lax.ppermute(confined[:, :, :1], 'pair', backward)]
    all_gather x0 -> x1, blocking collectives: none -> 57.4 us  [local(): grid_potential = lax.all_gather(potential, 'region', axis=0, tiled=True)]
    all_to_all x0 -> x1, blocking collectives: none -> 51.6 us  [local(): lax.all_to_all(parts, 'pair', split_axis=0, concat_axis=0, tiled=True)]
    another operation x2 -> x0, loops' own time: 41.5 us -> none  [the longest x1 41.2 us: local(): intersection_part, hamil_part = lax.map(pair_terms, pair_list)]
    all_to_all x2 -> x3, waiting for transfers between devices: 47.9 us -> 63.2 us  [the longest x1 41.1 us: local(): lax.all_to_all(applied, 'region', split_axis=1, concat_axis=0, tiled=True)]
    concatenate x1 -> x0, other arithmetic: 10.7 us -> none  [padded_2(): block = jnp.concatenate([low, block, high], axis=dim)]
  transfers between devices with their start and end apart: 10 -> 5, of which waited for: 8 -> 2; matrix products, arithmetic and copies ran while one was open for 2% -> 10% of each run, Pallas kernels for 0% -> 0%
where the time goes in v1:
time: 238 us; the launch traced here: 237 us
  blocking collectives  109 us (46%)
  waiting for transfers between devices  63.2 us (27%)
  local copies, waits for them, and re-layouts  23.1 us (10%)
  starting transfers between devices  16.1 us (7%)
  other arithmetic  14.5 us (6%)
  Pallas kernels  10.6 us (4%)
    all_gather x1, blocking collectives, local(): grid_potential = lax.all_gather(potential, 'region', axis=0, tiled=True)  57.4 us
    all_to_all x1, blocking collectives, local(): lax.all_to_all(parts, 'pair', split_axis=0, concat_axis=0, tiled=True)  51.6 us
    all_to_all x1, waiting for transfers between devices, local(): lax.all_to_all(applied, 'region', split_axis=1, concat_axis=0, tiled=True)  41.1 us
    all_to_all x1, waiting for transfers between devices, local(): lax.all_to_all(sums, 'region', split_axis=0, concat_axis=0, tiled=True)  22.1 us
    pallas_call x1, Pallas kernels, pair_blocks(): pl.pallas_call(pair_kernel, out_shape=jax.ShapeDtypeStruct((count, 2, W,...  10.6 us
    unnamed x15, local copies, waits for them, and re-layouts  8.7 us
    all_to_all x1, starting transfers between devices, local(): lax.all_to_all(confined, 'region', split_axis=1, concat_axis=0, tiled=True)  7.25 us
    convert_element_type x1, other arithmetic, local(): center = confined.astype(jnp.float32)  6.56 us
  transfers between devices with their start and end apart: 5, of which 2 were waited for; matrix products, arithmetic and copies ran while one was open for 10% of the time, Pallas kernels for 0%

profile of v1, /device:TPU:0, one launch (start us, length us, event | category | flops | bytes accessed | tf_op | source)
XLA Modules:
  0.0 237.4 jit_solution(11590331482733906952)
XLA Ops:
  0.6 0.0 copy-start
  0.7 0.6 copy-done
  1.3 0.6 gather_fusion
  2.0 6.6 %fusion.10 = (f32[128,8,8,128]{3,2,0,1:T(8,128)}, bf16[128,8,8,128]{3,2,0,1:T(8,128)(2,1)}) fusion(bf16[128,8,8,128]{3,2,1,0:T(8,128)(2,1)} %param.4, pred[128,8]{0,1:T(8,128)(4,1)S(1)} %broadcast_compare_fusion), kind=kLoop, calls=%fused_computation.28 | loop fusion | flops 2097152 | bytes 8389632 | tf_op jit(solution)/shard_map/convert_element_type | solution.py:61
  8.6 7.3 %all-to-all-start = ((bf16[128,8,8,128]{3,2,0,1:T(8,128)(2,1)}), bf16[128,8,8,128]{3,2,0,1:T(8,128)(2,1)S(1)}, u32[]{:S(2)}, u32[]{:S(2)}) async-start(bf16[128,8,8,128]{3,2,0,1:T(8,128)(2,1)} %get-tuple-element.16), calls=%async_computation | async-start | bytes 4194304 | tf_op jit(solution)/shard_map/all_to_all | solution.py:59
  15.8 3.3 %fusion.11 = (bf16[128,8,1,128]{3,2,0,1:T(2,128)(2,1)S(1)}, bf16[128,8,1,128]{3,2,0,1:T(2,128)(2,1)S(1)}) fusion(bf16[128,8,8,128]{3,2,0,1:T(8,128)(2,1)} %get-tuple-element.16), kind=kLoop, calls=%fused_computation.29 | loop fusion | bytes 1048576 | tf_op jit(solution)/shard_map/slice | solution.py:56
  19.2 0.3 copy.41
  19.5 0.7 collective-permute-start
  20.2 0.3 copy.43
  20.5 0.1 collective-permute-start.1
  20.6 2.8 %fusion.14 = (f32[128,7,8,128]{3,2,0,1:T(8,128)S(1)}, f32[128,7,8,128]{3,2,0,1:T(8,128)S(1)}) fusion(bf16[128,8,8,128]{3,2,0,1:T(8,128)(2,1)} %get-tuple-element.16), kind=kLoop, calls=%fused_computation.32 | loop fusion | bytes 14680064 | tf_op jit(solution)/shard_map/jit(_roll_static)/slice | solution.py:62
  23.3 0.0 copy-start.3
  23.4 3.2 %fusion.12 = (f32[128,8,7,128]{3,2,0,1:T(8,128)S(1)}, f32[128,8,7,128]{3,2,0,1:T(8,128)S(1)}) fusion(bf16[128,8,8,128]{3,2,0,1:T(8,128)(2,1)} %get-tuple-element.16), kind=kLoop, calls=%fused_computation.30 | loop fusion | bytes 14680064 | tf_op jit(solution)/shard_map/slice | solution.py:63
  26.6 57.4 %all_gather.3 = f32[8,8,128]{2,1,0:T(8,128)S(1)} all-gather(f32[1,8,128]{2,1,0:T(8,128)S(1)} %copy-done.3), channel_id=1, replica_groups=mesh['region'=8,'pair'=4] {'region'}, dimensions={0}, use_global_device_ids=true | all-gather | bytes 36864 | tf_op jit(solution)/shard_map/all_gather | solution.py:58
  84.0 1.1 fusion.13
  85.1 0.5 copy.42
  85.6 0.5 copy.44
  86.1 5.2 %fusion.5 = bf16[128,8,8,128]{3,2,0,1:T(8,128)(2,1)} fusion(f32[128,8,8,128]{3,2,0,1:T(8,128)S(1)} %copy-done.1, f32[128,1,8,128]{3,2,0,1:T(8,128)S(1)} %get-tuple-element.22, f32[128,7,8,128]{3,2,0,1:T(8,128)S(1)} %get-tuple-element.24, f32[128,7,8,128]{3,2,0,1:T(8,128)S(1)} %get-tuple-element.23, f32[128,1,8,128]{3,2,0,1:T(8,128)S(1)} %get-tuple-element.21, ...), kind=kLoop, calls=%fused_computation.8 | loop fusion | flops 16777216 | bytes 23105536 | tf_op jit(solution)/shard_map/convert_element_type | solution.py:69
  91.3 4.5 %all-to-all-start.1 = ((bf16[128,8,8,128]{3,2,0,1:T(8,128)(2,1)}), bf16[128,8,8,128]{3,2,0,1:T(8,128)(2,1)}, u32[]{:S(2)}, u32[]{:S(2)}) async-start(bf16[128,8,8,128]{3,2,0,1:T(8,128)(2,1)} %fusion.5), calls=%async_computation.1 | async-start | bytes 4194304 | tf_op jit(solution)/shard_map/all_to_all | solution.py:70
  95.8 0.1 copy.46.pairs_ref
  95.9 2.2 copy.60
  98.1 41.1 %all-to-all-done.1 = bf16[128,8,8,128]{3,2,0,1:T(8,128)(2,1)} async-done(((bf16[128,8,8,128]{3,2,0,1:T(8,128)(2,1)}), bf16[128,8,8,128]{3,2,0,1:T(8,128)(2,1)}, u32[]{:S(2)}, u32[]{:S(2)}) %all-to-all-start.1) | async-done | bytes 2097184 | tf_op jit(solution)/shard_map/all_to_all | solution.py:70
  139.2 2.2 copy.59
  141.4 10.6 %shard_map.67 = f32[32,2,128,128]{3,2,1,0:T(8,128)S(1)} custom-call(s32[32,2]{1,0:T(8,128)S(1)} %copy.46.pairs_ref, bf16[1024,1024]{1,0:T(8,128)(2,1)S(1)} %bitcast.37, bf16[1024,1024]{1,0:T(8,128)(2,1)S(1)} %bitcast.38), custom_call_target="tpu_custom_call" | custom-call | flops 2147483648 | bytes 8388608 | tf_op jit(solution)/shard_map/pallas_call | solution.py:28
  152.1 51.6 %all_to_all.40 = f32[4,8,2,128,128]{4,3,2,1,0:T(8,128)} all-to-all(f32[4,8,2,128,128]{4,3,2,1,0:T(8,128)S(1)} %bitcast.36), channel_id=1, replica_groups=mesh['region'=8,'pair'=4] {'pair'}, dimensions={0} | all-to-all | bytes 8388608 | tf_op jit(solution)/shard_map/all_to_all | solution.py:77
  203.7 2.7 %reduce_sum.18 = f32[8,2,128,128]{3,2,1,0:T(8,128)S(1)} reduce(f32[4,8,2,128,128]{4,3,2,1,0:T(8,128)} %all_to_all.40, f32[]{:T(128)} %constant.35.clone.1), dimensions={0}, to_apply=%region_0.1 | reduce | flops 786432 | bytes 5242884 | tf_op jit(solution)/shard_map/reduce_sum | solution.py:78
  206.3 1.1 copy.47
  207.5 3.6 %all-to-all-start.3 = ((f32[8,2,8,16,128]{4,3,1,2,0:T(8,128)}), f32[8,2,8,16,128]{4,3,1,2,0:T(8,128)S(1)}, u32[]{:S(2)}, u32[]{:S(2)}) async-start(f32[8,2,8,16,128]{4,3,1,2,0:T(8,128)} %copy.47), calls=%async_computation.3 | async-start | bytes 2097152 | tf_op jit(solution)/shard_map/all_to_all | solution.py:80
  211.0 3.5 %copy.48 = bf16[128,8,8,128]{3,2,1,0:T(8,128)(2,1)} copy(bf16[128,8,8,128]{3,2,0,1:T(8,128)(2,1)} %fusion.5) | data formatting | bytes 4194304
  214.5 22.1 %all-to-all-done.3 = f32[8,2,8,16,128]{4,3,1,2,0:T(8,128)S(1)} async-done(((f32[8,2,8,16,128]{4,3,1,2,0:T(8,128)}), f32[8,2,8,16,128]{4,3,1,2,0:T(8,128)S(1)}, u32[]{:S(2)}, u32[]{:S(2)}) %all-to-all-start.3) | async-done | bytes 1048608 | tf_op jit(solution)/shard_map/all_to_all | solution.py:80
  236.6 0.1 reduce_sum.19
  236.7 0.7 copy_bitcast_fusion.2
  (16 shorter events, 0.1 us)
Async XLA Ops:
  0.6 0.7 copy-start
  8.6 82.7 %all-to-all-start = ((bf16[128,8,8,128]{3,2,0,1:T(8,128)(2,1)}), bf16[128,8,8,128]{3,2,0,1:T(8,128)(2,1)S(1)}, u32[]{:S(2)}, u32[]{:S(2)}) async-start(bf16[128,8,8,128]{3,2,0,1:T(8,128)(2,1)} %get-tuple-element.16), calls=%async_computation | async-start | bytes 4194304 | tf_op jit(solution)/shard_map/all_to_all | solution.py:59
  19.5 65.6 %collective-permute-start = (bf16[128,8,1,128]{3,1,2,0:T(8,128)(2,1)S(1)}, bf16[128,8,1,128]{3,1,2,0:T(8,128)(2,1)S(1)}, u32[]{:S(2)}, u32[]{:S(2)}) collective-permute-start(bf16[128,8,1,128]{3,1,2,0:T(8,128)(2,1)S(1)} %copy.41), channel_id=1, source_target_pairs={{1,0},{2,1},{3,2},{0,3},{5,4},{6,5},{7,6},{4,7},{9,8},{10,9},{11,1... | collective-permute-start | bytes 786440 | tf_op jit(solution)/shard_map/ppermute | solution.py:57
  20.5 65.1 %collective-permute-start.1 = (bf16[128,8,1,128]{3,1,2,0:T(8,128)(2,1)S(1)}, bf16[128,8,1,128]{3,1,2,0:T(8,128)(2,1)S(1)}, u32[]{:S(2)}, u32[]{:S(2)}) collective-permute-start(bf16[128,8,1,128]{3,1,2,0:T(8,128)(2,1)S(1)} %copy.43), channel_id=1, source_target_pairs={{0,1},{1,2},{2,3},{3,0},{4,5},{5,6},{6,7},{7,4},{8,9},{9,10},{10,1... | collective-permute-start | bytes 786440 | tf_op jit(solution)/shard_map/ppermute | solution.py:56
  23.3 3.2 %copy-start.3 = (f32[1,8,128]{2,1,0:T(8,128)S(1)}, f32[1,8,128]{2,1,0:T(8,128)}, u32[]{:S(2)}) copy-start(f32[1,8,128]{2,1,0:T(8,128)} %param.5) | copy-start | bytes 12292
  23.4 62.7 %copy-start.1 = (f32[128,8,8,128]{3,2,0,1:T(8,128)S(1)}, f32[128,8,8,128]{3,2,0,1:T(8,128)}, u32[]{:S(2)}) copy-start(f32[128,8,8,128]{3,2,0,1:T(8,128)} %get-tuple-element.15) | copy-start | bytes 12582916
  91.3 4.5 %copy-start.4 = (s32[32,2]{0,1:T(2,128)S(1)}, s32[32,2]{0,1:T(2,128)}, u32[]{:S(2)}) copy-start(s32[32,2]{0,1:T(2,128)} %param.6) | copy-start | bytes 772
  91.3 4.6 %copy-start.2 = (bf16[128,8,8,128]{3,2,0,1:T(8,128)(2,1)}, bf16[128,8,8,128]{3,2,0,1:T(8,128)(2,1)S(1)}, u32[]{:S(2)}) copy-start(bf16[128,8,8,128]{3,2,0,1:T(8,128)(2,1)S(1)} %all-to-all-done) | copy-start | bytes 6291460
  91.3 47.9 %all-to-all-start.1 = ((bf16[128,8,8,128]{3,2,0,1:T(8,128)(2,1)}), bf16[128,8,8,128]{3,2,0,1:T(8,128)(2,1)}, u32[]{:S(2)}, u32[]{:S(2)}) async-start(bf16[128,8,8,128]{3,2,0,1:T(8,128)(2,1)} %fusion.5), calls=%async_computation.1 | async-start | bytes 4194304 | tf_op jit(solution)/shard_map/all_to_all | solution.py:70
  207.5 29.2 %all-to-all-start.3 = ((f32[8,2,8,16,128]{4,3,1,2,0:T(8,128)}), f32[8,2,8,16,128]{4,3,1,2,0:T(8,128)S(1)}, u32[]{:S(2)}, u32[]{:S(2)}) async-start(f32[8,2,8,16,128]{4,3,1,2,0:T(8,128)} %copy.47), calls=%async_computation.3 | async-start | bytes 2097152 | tf_op jit(solution)/shard_map/all_to_all | solution.py:80

commit v2 on v1

--- a/solution.py
+++ b/solution.py
@@ -8,26 +8,24 @@
 W = 128
 
 
-def pair_kernel(pairs_ref, data_ref, applied_ref, out_ref):
+def pair_kernel(pairs_ref, data_ref, right_ref, out_ref):
     contract = (((1,), (1,)), ((), ()))
 
     def step(k, carry):
         left = data_ref[pl.ds(pl.multiple_of(pairs_ref[k, 0] * W, W), W), :]
         rows = pl.ds(pl.multiple_of(pairs_ref[k, 1] * W, W), W)
-        right = jnp.concatenate([data_ref[rows, :], applied_ref[rows, :]], axis=0)
-        both = lax.dot_general(left, right, contract, preferred_element_type=jnp.float32)
-        out_ref[k, 0] = both[:, :W]
-        out_ref[k, 1] = both[:, W:]
+        right = right_ref[rows, :]
+        out_ref[k] = lax.dot_general(left, right, contract, preferred_element_type=jnp.float32)
         return carry
 
     lax.fori_loop(0, pairs_ref.shape[0], step, 0)
 
 
-def pair_blocks(pair_list, data, applied):
+def pair_blocks(pair_list, data, right):
     count = pair_list.shape[0]
     return pl.pallas_call(
         pair_kernel,
-        out_shape=jax.ShapeDtypeStruct((count, 2, W, W), jnp.float32),
+        out_shape=jax.ShapeDtypeStruct((count, W, W), jnp.float32),
         in_specs=[
             pl.BlockSpec(memory_space=pltpu.SMEM),
             pl.BlockSpec(memory_space=pltpu.VMEM),
@@ -36,11 +34,36 @@
         out_specs=pl.BlockSpec(memory_space=pltpu.VMEM),
         compiler_params=pltpu.CompilerParams(vmem_limit_bytes=32 * 2**20),
         cost_estimate=pl.CostEstimate(
-            flops=count * 4 * W * W * data.shape[1],
-            bytes_accessed=data.size * 4 + count * 8 * W * W,
+            flops=count * 2 * W * W * data.shape[1],
+            bytes_accessed=data.size * 4 + count * 4 * W * W,
             transcendentals=0,
         ),
-    )(pair_list, data, applied)
+    )(pair_list, data, right)
+
+
+def halved(parts, bit):
+    count = lax.axis_size("pair")
+    mine = (lax.axis_index("pair") // bit) % 2
+    kept = lax.dynamic_index_in_dim(parts, mine, 0, keepdims=False)
+    given = lax.dynamic_index_in_dim(parts, 1 - mine, 0, keepdims=False)
+    return kept + lax.ppermute(given, "pair", [(i, i ^ bit) for i in range(count)])
+
+
+def reduced(blocks):
+    count = lax.axis_size("pair")
+    region_count = lax.axis_size("region")
+    listed = blocks.shape[0] // count
+    parts = blocks.reshape(count, listed, W, W)
+    bit = 1
+    while bit < count:
+        rest = parts.shape[0] // 2
+        parts = parts.reshape(rest, 2, listed, W, W).swapaxes(0, 1)
+        parts = halved(parts, bit)
+        bit *= 2
+    width = W // region_count
+    sums = parts.reshape(listed, region_count, width, W).swapaxes(0, 1)
+    sums = lax.all_to_all(sums, "region", split_axis=0, concat_axis=0, tiled=True)
+    return jnp.sum(sums, axis=0).reshape(listed, width * W)
 
 
 def local(phi, potential, pair_list, support):
@@ -56,7 +79,10 @@
     low = lax.ppermute(confined[:, :, -1:], "pair", forward)
     high = lax.ppermute(confined[:, :, :1], "pair", backward)
     grid_potential = lax.all_gather(potential, "region", axis=0, tiled=True)
-    data = lax.all_to_all(confined, "region", split_axis=1, concat_axis=0, tiled=True)
+    low, high, grid_potential, sent = lax.optimization_barrier(
+        (low, high, grid_potential, confined)
+    )
+    data = lax.all_to_all(sent, "region", split_axis=1, concat_axis=0, tiled=True)
 
     center = confined.astype(jnp.float32)
     total = jnp.roll(center, -1, axis=1) + jnp.roll(center, 1, axis=1) - 6.0 * center
@@ -70,16 +96,11 @@
     applied_data = lax.all_to_all(applied, "region", split_axis=1, concat_axis=0, tiled=True)
 
     flat = (func_count * region_count, -1)
-    blocks = pair_blocks(pair_list, data.reshape(flat), applied_data.reshape(flat))
-    listed = pair_list.shape[0] // pair_axis
-    width = W // region_count
-    parts = blocks.reshape(pair_axis, listed, 2, W, W)
-    parts = lax.all_to_all(parts, "pair", split_axis=0, concat_axis=0, tiled=True)
-    sums = jnp.sum(parts, axis=0)
-    sums = sums.reshape(listed, 2, region_count, width, W).transpose(2, 1, 0, 3, 4)
-    sums = lax.all_to_all(sums, "region", split_axis=0, concat_axis=0, tiled=True)
-    result = jnp.sum(sums, axis=0).reshape(2, listed, width * W)
-    return result[0], result[1], applied
+    data = data.reshape(flat)
+    applied_data = applied_data.reshape(flat)
+    intersection = reduced(pair_blocks(pair_list, data, data))
+    hamiltonian = reduced(pair_blocks(pair_list, data, applied_data))
+    return intersection, hamiltonian, applied
 
 
 def solution(mesh):

time: 238 us -> 230 us (0.966)
  blocking collectives: 109 us -> 31.5 us
  waiting for transfers between devices: 63.2 us -> 120 us
  Pallas kernels: 10.6 us -> 16.3 us
  starting transfers between devices: 16.1 us -> 21.7 us
  local copies, waits for them, and re-layouts: 23.1 us -> 27 us
    all_to_all x1 -> x0, blocking collectives: 51.6 us -> none  [local(): lax.all_to_all(parts, 'pair', split_axis=0, concat_axis=0, tiled=True)]
    all_to_all x2 -> x3, waiting for transfers between devices: 22.1 us -> 52.8 us  [the longest x1 42.7 us: local(): lax.all_to_all(sent, 'region', split_axis=1, concat_axis=0, tiled=True)]
    ppermute x0 -> x4, waiting for transfers between devices: none -> 26.9 us  [halved(): lax.ppermute(given, 'pair', [(i, i ^ bit) for i in range(count)])]
    all_gather x1, blocking collectives: 57.4 us -> 31.5 us  [local(): grid_potential = lax.all_gather(potential, 'region', axis=0, tiled=True)]
    pallas_call x1 -> x2, Pallas kernels: 10.6 us -> 16.3 us  [pair_blocks(): pl.pallas_call(pair_kernel, out_shape=jax.ShapeDtypeStruct((count, W, W),...]
    unnamed x15 -> x28, local copies, waits for them, and re-layouts: 8.7 us -> 13.9 us
    convert_element_type x1, other arithmetic: 6.56 us -> 2.11 us  [local(): center = confined.astype(jnp.float32)]
    add x0 -> x4, other arithmetic: none -> 4.05 us  [halved(): kept + lax.ppermute(given, 'pair', [(i, i ^ bit) for i in range(count)])]
  transfers between devices with their start and end apart: 5 -> 10, of which waited for: 2 -> 5; matrix products, arithmetic and copies ran while one was open for 10% -> 9% of each run, Pallas kernels for 0% -> 4%
where the time goes in v2:
time: 230 us
  waiting for transfers between devices  120 us (52%)
  blocking collectives  31.5 us (14%)
  local copies, waits for them, and re-layouts  27 us (12%)
  starting transfers between devices  21.7 us (9%)
  Pallas kernels  16.3 us (7%)
  other arithmetic  12.2 us (5%)
    all_to_all x1, waiting for transfers between devices, local(): lax.all_to_all(sent, 'region', split_axis=1, concat_axis=0, tiled=True)  42.7 us
    all_to_all x1, waiting for transfers between devices, local(): lax.all_to_all(applied, 'region', split_axis=1, concat_axis=0, tiled=True)  40.6 us
    all_gather x1, blocking collectives, local(): grid_potential = lax.all_gather(potential, 'region', axis=0, tiled=True)  31.5 us
    ppermute x4, waiting for transfers between devices, halved(): lax.ppermute(given, 'pair', [(i, i ^ bit) for i in range(count)])  26.9 us
    pallas_call x2, Pallas kernels, pair_blocks(): pl.pallas_call(pair_kernel, out_shape=jax.ShapeDtypeStruct((count, W, W),...  16.3 us
    unnamed x28, local copies, waits for them, and re-layouts  13.9 us
    all_to_all x2, waiting for transfers between devices, reduced(): lax.all_to_all(sums, 'region', split_axis=0, concat_axis=0, tiled=True)  10 us
    all_to_all x2, starting transfers between devices, reduced(): lax.all_to_all(sums, 'region', split_axis=0, concat_axis=0, tiled=True)  9.13 us
  transfers between devices with their start and end apart: 10, of which 5 were waited for; matrix products, arithmetic and copies ran while one was open for 9% of the time, Pallas kernels for 4%

profile of v2, /device:TPU:0, one launch (start us, length us, event | category | flops | bytes accessed | tf_op | source)
XLA Modules:
  0.0 229.8 jit_solution(7927229071603393525)
XLA Ops:
  2.0 2.1 fusion.10
  4.7 2.0 collective-permute-start.1
  6.7 1.1 fusion.13
  7.8 3.4 %fusion.11 = (f32[128,8,7,128]{3,1,2,0:T(8,128)}, f32[128,8,7,128]{3,1,2,0:T(8,128)}) fusion(bf16[128,8,8,128]{3,1,2,0:T(8,128)(2,1)S(1)} %get-tuple-element.7), kind=kLoop, calls=%fused_computation.35 | loop fusion | bytes 14680064 | tf_op jit(solution)/shard_map/slice | solution.py:89
  11.3 31.5 %all_gather.3 = f32[8,8,128]{2,1,0:T(8,128)S(1)} all-gather(f32[1,8,128]{2,1,0:T(8,128)S(1)} %copy-done.9), channel_id=1, replica_groups=mesh['region'=8,'pair'=4] {'region'}, dimensions={0}, use_global_device_ids=true | all-gather | bytes 36864 | tf_op jit(solution)/shard_map/all_gather | solution.py:81
  43.5 5.8 %fusion.5 = bf16[128,8,8,128]{3,1,2,0:T(8,128)(2,1)S(1)} fusion(f32[128,8,8,128]{3,1,2,0:T(8,128)S(1)} %get-tuple-element.17, f32[128,1,8,128]{3,1,2,0:T(1,128)S(1)} %get-tuple-element.22, f32[128,7,8,128]{3,1,2,0:T(8,128)S(1)} %get-tuple-element.24, f32[128,7,8,128]{3,1,2,0:T(8,128)S(1)} %get-tuple-element.23, f32[128,1,8,128]{3,1,2,0:T(1,128)S(1)} %get-tuple-element.21, ...), kind=kLoop, calls=%fused_computation.8 | loop fusion | flops 16777216 | bytes 23105536 | tf_op jit(solution)/shard_map/convert_element_type | solution.py:95
  49.4 1.3 copy-done.6
  50.7 1.7 copy.26
  52.4 5.5 %all-to-all-start.2 = ((bf16[128,8,8,128]{3,2,0,1:T(8,128)(2,1)}), bf16[128,8,8,128]{3,2,0,1:T(8,128)(2,1)}, u32[]{:S(2)}, u32[]{:S(2)}) async-start(bf16[128,8,8,128]{3,2,0,1:T(8,128)(2,1)} %copy.26), calls=%async_computation.2 | async-start | bytes 4194304 | tf_op jit(solution)/shard_map/all_to_all | solution.py:96
  57.9 1.7 copy.21
  59.5 40.6 %all-to-all-done.2 = bf16[128,8,8,128]{3,2,0,1:T(8,128)(2,1)} async-done(((bf16[128,8,8,128]{3,2,0,1:T(8,128)(2,1)}), bf16[128,8,8,128]{3,2,0,1:T(8,128)(2,1)}, u32[]{:S(2)}, u32[]{:S(2)}) %all-to-all-start.2) | async-done | bytes 2097184 | tf_op jit(solution)/shard_map/all_to_all | solution.py:96
  100.1 3.6 %all-to-all-start = ((bf16[128,8,8,128]{3,2,0,1:T(8,128)(2,1)}), bf16[128,8,8,128]{3,2,0,1:T(8,128)(2,1)S(1)}, u32[]{:S(2)}, u32[]{:S(2)}) async-start(bf16[128,8,8,128]{3,2,0,1:T(8,128)(2,1)} %copy.21), calls=%async_computation | async-start | bytes 4194304 | tf_op jit(solution)/shard_map/all_to_all | solution.py:85
  103.8 3.6 %copy.43 = bf16[128,8,8,128]{3,1,2,0:T(8,128)(2,1)} copy(bf16[128,8,8,128]{3,2,1,0:T(8,128)(2,1)} %bitcast.27) | data formatting | bytes 4194304
  107.4 42.7 %all-to-all-done = bf16[128,8,8,128]{3,2,0,1:T(8,128)(2,1)S(1)} async-done(((bf16[128,8,8,128]{3,2,0,1:T(8,128)(2,1)}), bf16[128,8,8,128]{3,2,0,1:T(8,128)(2,1)S(1)}, u32[]{:S(2)}, u32[]{:S(2)}) %all-to-all-start) | async-done | bytes 2097184 | tf_op jit(solution)/shard_map/all_to_all | solution.py:85
  150.1 1.3 copy-done.8
  151.5 2.4 %copy.44 = bf16[128,8,8,128]{3,1,2,0:T(8,128)(2,1)S(1)} copy(bf16[128,8,8,128]{3,2,1,0:T(8,128)(2,1)} %bitcast.52) | data formatting | bytes 4194304
  153.8 8.2 %shard_map.68 = f32[32,128,128]{2,1,0:T(8,128)S(1)} custom-call(s32[32,2]{1,0:T(8,128)S(1)} %copy.22.pairs_ref, bf16[1024,1024]{1,0:T(8,128)(2,1)S(1)} %bitcast.44, bf16[1024,1024]{1,0:T(8,128)(2,1)S(1)} %bitcast.51), custom_call_target="tpu_custom_call" | custom-call | flops 1073741824 | bytes 6291456 | tf_op jit(solution)/shard_map/pallas_call | solution.py:26
  162.1 1.3 copy-done.1
  163.6 8.1 %shard_map.67 = f32[32,128,128]{2,1,0:T(8,128)S(1)} custom-call(s32[32,2]{1,0:T(8,128)S(1)} %copy.22.pairs_ref, bf16[1024,1024]{1,0:T(8,128)(2,1)S(1)} %bitcast.45, bf16[1024,1024]{1,0:T(8,128)(2,1)S(1)} %bitcast.46), custom_call_target="tpu_custom_call" | custom-call | flops 1073741824 | bytes 6291456 | tf_op jit(solution)/shard_map/pallas_call | solution.py:26
  171.7 1.2 dynamic-slice_bitcast_fusion.1
  173.5 1.4 bitcast_add_fusion
  174.9 0.8 constant_dynamic-slice_fusion
  175.8 14.2 %collective-permute-done.5 = f32[1,8,128,128]{3,2,1,0:T(8,128)} collective-permute-done((f32[1,8,128,128]{3,2,1,0:T(8,128)}, f32[1,8,128,128]{3,2,1,0:T(8,128)}, u32[]{:S(2)}, u32[]{:S(2)}) %collective-permute-start.5) | collective-permute-done | bytes 524320 | tf_op jit(solution)/shard_map/ppermute | solution.py:49
  189.9 1.1 dynamic-slice_add_fusion
  191.0 0.8 copy.28
  191.9 3.5 %all-to-all-start.3 = ((f32[8,8,16,128]{3,2,1,0:T(8,128)}), f32[8,8,16,128]{3,2,1,0:T(8,128)S(1)}, u32[]{:S(2)}, u32[]{:S(2)}) async-start(f32[8,8,16,128]{3,2,1,0:T(8,128)} %copy.28), calls=%async_computation.3 | async-start | bytes 1048576 | tf_op jit(solution)/shard_map/all_to_all | solution.py:65
  195.4 1.4 bitcast_add_fusion.1
  197.2 12.7 %collective-permute-done.3 = f32[1,8,128,128]{3,2,1,0:T(8,128)S(1)} collective-permute-done((f32[1,8,128,128]{3,2,1,0:T(8,128)S(1)}, f32[1,8,128,128]{3,2,1,0:T(8,128)S(1)}, u32[]{:S(2)}, u32[]{:S(2)}) %collective-permute-start.3) | collective-permute-done | bytes 524320 | tf_op jit(solution)/shard_map/ppermute | solution.py:49
  210.0 0.8 copy.23
  210.9 5.6 %all-to-all-start.1 = ((f32[8,8,16,128]{3,2,1,0:T(8,128)}), f32[8,8,16,128]{3,2,1,0:T(8,128)S(1)}, u32[]{:S(2)}, u32[]{:S(2)}) async-start(f32[8,8,16,128]{3,2,1,0:T(8,128)} %copy.23), calls=%async_computation.1 | async-start | bytes 1048576 | tf_op jit(solution)/shard_map/all_to_all | solution.py:65
  216.5 1.9 copy.30
  219.1 10.0 %all-to-all-done.1 = f32[8,8,16,128]{3,2,1,0:T(8,128)S(1)} async-done(((f32[8,8,16,128]{3,2,1,0:T(8,128)}), f32[8,8,16,128]{3,2,1,0:T(8,128)S(1)}, u32[]{:S(2)}, u32[]{:S(2)}) %all-to-all-start.1) | async-done | bytes 524320 | tf_op jit(solution)/shard_map/all_to_all | solution.py:65
  (47 shorter events, 5.4 us)
Async XLA Ops:
  0.6 0.7 copy-start
  4.2 39.2 %collective-permute-start = (bf16[128,8,1,128]{3,1,2,0:T(8,128)(2,1)S(1)}, bf16[128,8,1,128]{3,1,2,0:T(8,128)(2,1)S(1)}, u32[]{:S(2)}, u32[]{:S(2)}) collective-permute-start(bf16[128,8,1,128]{3,1,2,0:T(8,128)(2,1)S(1)} %get-tuple-element.26), channel_id=1, source_target_pairs={{0,1},{1,2},{2,3},{3,0},{4,5},{5,6},{6,7},{7,4},{8,9},{9,10},{10,1... | collective-permute-start | bytes 786440 | tf_op jit(solution)/shard_map/ppermute | solution.py:79
  4.7 38.7 %collective-permute-start.1 = (bf16[128,8,1,128]{3,1,2,0:T(8,128)(2,1)S(1)}, bf16[128,8,1,128]{3,1,2,0:T(8,128)(2,1)S(1)}, u32[]{:S(2)}, u32[]{:S(2)}) collective-permute-start(bf16[128,8,1,128]{3,1,2,0:T(8,128)(2,1)S(1)} %get-tuple-element.25), channel_id=1, source_target_pairs={{1,0},{2,1},{3,2},{0,3},{5,4},{6,5},{7,6},{4,7},{9,8},{10,9},{11,1... | collective-permute-start | bytes 786440 | tf_op jit(solution)/shard_map/ppermute | solution.py:80
  7.8 3.4 %copy-start.9 = (f32[1,8,128]{2,1,0:T(8,128)S(1)}, f32[1,8,128]{2,1,0:T(8,128)}, u32[]{:S(2)}) copy-start(f32[1,8,128]{2,1,0:T(8,128)} %param.5) | copy-start | bytes 12292
  49.4 1.3 copy-start.6
  52.4 47.7 %all-to-all-start.2 = ((bf16[128,8,8,128]{3,2,0,1:T(8,128)(2,1)}), bf16[128,8,8,128]{3,2,0,1:T(8,128)(2,1)}, u32[]{:S(2)}, u32[]{:S(2)}) async-start(bf16[128,8,8,128]{3,2,0,1:T(8,128)(2,1)} %copy.26), calls=%async_computation.2 | async-start | bytes 4194304 | tf_op jit(solution)/shard_map/all_to_all | solution.py:96
  57.9 45.9 %copy-start.10 = (s32[32,2]{0,1:T(2,128)S(1)}, s32[32,2]{0,1:T(2,128)}, u32[]{:S(2)}) copy-start(s32[32,2]{0,1:T(2,128)} %param.6) | copy-start | bytes 772
  100.1 50.0 %all-to-all-start = ((bf16[128,8,8,128]{3,2,0,1:T(8,128)(2,1)}), bf16[128,8,8,128]{3,2,0,1:T(8,128)(2,1)S(1)}, u32[]{:S(2)}, u32[]{:S(2)}) async-start(bf16[128,8,8,128]{3,2,0,1:T(8,128)(2,1)} %copy.21), calls=%async_computation | async-start | bytes 4194304 | tf_op jit(solution)/shard_map/all_to_all | solution.py:85
  150.1 1.3 copy-start.8
  151.5 2.4 %copy-start.5 = (bf16[128,8,8,128]{3,1,2,0:T(8,128)(2,1)S(1)}, bf16[128,8,8,128]{3,1,2,0:T(8,128)(2,1)}, u32[]{:S(2)}) copy-start(bf16[128,8,8,128]{3,1,2,0:T(8,128)(2,1)} %copy.43) | copy-start | bytes 6291460
  162.1 1.3 copy-start.1
  163.5 10.0 %collective-permute-start.4 = (f32[2,8,128,128]{3,2,1,0:T(8,128)S(1)}, f32[2,8,128,128]{3,2,1,0:T(8,128)}, u32[]{:S(2)}, u32[]{:S(2)}) collective-permute-start(f32[2,8,128,128]{3,2,1,0:T(8,128)S(1)} %dynamic-slice_bitcast_fusion), channel_id=1, source_target_pairs={{0,1},{1,0},{2,3},{3,2},{4,5},{5,4},{6,7},{7,6},{8,9},{9,8},{10,11... | collective-permute-start | bytes 3145736 | tf_op jit(solution)/shard_map/ppermute | solution.py:49
  163.6 9.9 %copy-start.2 = (f32[32,128,128]{2,1,0:T(8,128)S(1)}, f32[32,128,128]{2,1,0:T(8,128)}, u32[]{:S(2)}) copy-start(f32[32,128,128]{2,1,0:T(8,128)} %copy-done.1) | copy-start | bytes 6291460
  171.7 3.2 %copy-start.3 = (f32[32,128,128]{2,1,0:T(8,128)}, f32[32,128,128]{2,1,0:T(8,128)S(1)}, u32[]{:S(2)}) copy-start(f32[32,128,128]{2,1,0:T(8,128)S(1)} %shard_map.67) | copy-start | bytes 6291460
  172.9 22.5 %collective-permute-start.2 = (f32[2,8,128,128]{3,2,1,0:T(8,128)}, f32[2,8,128,128]{3,2,1,0:T(8,128)}, u32[]{:S(2)}, u32[]{:S(2)}) collective-permute-start(f32[2,8,128,128]{3,2,1,0:T(8,128)} %dynamic-slice_bitcast_fusion.1), channel_id=1, source_target_pairs={{0,1},{1,0},{2,3},{3,2},{4,5},{5,4},{6,7},{7,6},{8,9},{9,8},{10,11... | collective-permute-start | bytes 3145736 | tf_op jit(solution)/shard_map/ppermute | solution.py:49
  175.7 19.6 %copy-start.4 = (f32[32,128,128]{2,1,0:T(8,128)S(1)}, f32[32,128,128]{2,1,0:T(8,128)}, u32[]{:S(2)}) copy-start(f32[32,128,128]{2,1,0:T(8,128)} %copy-done.3) | copy-start | bytes 6291460
  175.8 14.2 %collective-permute-start.5 = (f32[1,8,128,128]{3,2,1,0:T(8,128)}, f32[1,8,128,128]{3,2,1,0:T(8,128)}, u32[]{:S(2)}, u32[]{:S(2)}) collective-permute-start(f32[1,8,128,128]{3,2,1,0:T(8,128)} %constant_dynamic-slice_fusion), channel_id=1, source_target_pairs={{0,2},{1,3},{2,0},{3,1},{4,6},{5,7},{6,4},{7,5},{8,10},{9,11},{10,... | collective-permute-start | bytes 1572872 | tf_op jit(solution)/shard_map/ppermute | solution.py:49
  191.9 19.0 %all-to-all-start.3 = ((f32[8,8,16,128]{3,2,1,0:T(8,128)}), f32[8,8,16,128]{3,2,1,0:T(8,128)S(1)}, u32[]{:S(2)}, u32[]{:S(2)}) async-start(f32[8,8,16,128]{3,2,1,0:T(8,128)} %copy.28), calls=%async_computation.3 | async-start | bytes 1048576 | tf_op jit(solution)/shard_map/all_to_all | solution.py:65
  196.8 19.7 %copy-start.7 = (bf16[128,8,8,128]{3,1,2,0:T(8,128)(2,1)S(1)}, bf16[128,8,8,128]{3,1,2,0:T(8,128)(2,1)}, u32[]{:S(2)}) copy-start(bf16[128,8,8,128]{3,1,2,0:T(8,128)(2,1)} %copy-done.6) | copy-start | bytes 6291460
  196.9 13.1 %collective-permute-start.3 = (f32[1,8,128,128]{3,2,1,0:T(8,128)S(1)}, f32[1,8,128,128]{3,2,1,0:T(8,128)S(1)}, u32[]{:S(2)}, u32[]{:S(2)}) collective-permute-start(f32[1,8,128,128]{3,2,1,0:T(8,128)S(1)} %constant_dynamic-slice_fusion.1), channel_id=1, source_target_pairs={{0,2},{1,3},{2,0},{3,1},{4,6},{5,7},{6,4},{7,5},{8,10},{9,11},{10,... | collective-permute-start | bytes 1572872 | tf_op jit(solution)/shard_map/ppermute | solution.py:49
  210.9 18.3 %all-to-all-start.1 = ((f32[8,8,16,128]{3,2,1,0:T(8,128)}), f32[8,8,16,128]{3,2,1,0:T(8,128)S(1)}, u32[]{:S(2)}, u32[]{:S(2)}) async-start(f32[8,8,16,128]{3,2,1,0:T(8,128)} %copy.23), calls=%async_computation.1 | async-start | bytes 1048576 | tf_op jit(solution)/shard_map/all_to_all | solution.py:65

commit v3 on v2

--- a/solution.py
+++ b/solution.py
@@ -41,6 +41,20 @@
     )(pair_list, data, right)
 
 
+def gathered(block):
+    count = lax.axis_size("region")
+    index = lax.axis_index("region")
+    bit = 1
+    while bit < count:
+        other = lax.ppermute(block, "region", [(i, i ^ bit) for i in range(count)])
+        upper = (index // bit) % 2 == 1
+        block = jnp.concatenate(
+            [jnp.where(upper, other, block), jnp.where(upper, block, other)], axis=0
+        )
+        bit *= 2
+    return block
+
+
 def halved(parts, bit):
     count = lax.axis_size("pair")
     mine = (lax.axis_index("pair") // bit) % 2
@@ -78,7 +92,7 @@
     backward = [(target, source) for source, target in forward]
     low = lax.ppermute(confined[:, :, -1:], "pair", forward)
     high = lax.ppermute(confined[:, :, :1], "pair", backward)
-    grid_potential = lax.all_gather(potential, "region", axis=0, tiled=True)
+    grid_potential = gathered(potential)
     low, high, grid_potential, sent = lax.optimization_barrier(
         (low, high, grid_potential, confined)
     )
@@ -93,7 +107,8 @@
     total = total + z_padded[..., 2:] + z_padded[..., :-2]
     keep = live.astype(jnp.float32)[:, :, None, None]
     applied = ((-0.5 * total + grid_potential[None] * center) * keep).astype(jnp.bfloat16)
-    applied_data = lax.all_to_all(applied, "region", split_axis=1, concat_axis=0, tiled=True)
+    data, applied_sent = lax.optimization_barrier((data, applied))
+    applied_data = lax.all_to_all(applied_sent, "region", split_axis=1, concat_axis=0, tiled=True)
 
     flat = (func_count * region_count, -1)
     data = data.reshape(flat)

time: 230 us -> 210 us (0.913)
  blocking collectives: 31.5 us -> 0 us
  starting transfers between devices: 21.7 us -> 29.8 us
  other arithmetic: 12.2 us -> 17.6 us
    all_gather x1 -> x0, blocking collectives: 31.5 us -> none  [local(): grid_potential = lax.all_gather(potential, 'region', axis=0, tiled=True)]
    ppermute x1, waiting for transfers between devices: 0.01 us -> 10.6 us  [local(): low = lax.ppermute(confined[:, :, -1:], 'pair', forward)]
    ppermute x0 -> x3, starting transfers between devices: none -> 7.76 us  [gathered(): other = lax.ppermute(block, 'region', [(i, i ^ bit) for i in range(count)])]
    all_to_all x1, waiting for transfers between devices: 42.7 us -> 36 us  [local(): lax.all_to_all(sent, 'region', split_axis=1, concat_axis=0, tiled=True)]
    convert_element_type x1, other arithmetic: 2.11 us -> 6.51 us  [local(): center = confined.astype(jnp.float32)]
    all_to_all x1, waiting for transfers between devices: 40.6 us -> 36.5 us  [local(): lax.all_to_all(applied_sent, 'region', split_axis=1, concat_axis=0, tiled...]
    unnamed x28 -> x22, local copies, waits for them, and re-layouts: 13.9 us -> 10.7 us
    slice x1, local copies, waits for them, and re-layouts: 0.07 us -> 3.27 us  [local(): high = lax.ppermute(confined[:, :, :1], 'pair', backward)]
  transfers between devices with their start and end apart: 10 -> 13, of which waited for: 5 -> 8; matrix products, arithmetic and copies ran while one was open for 9% -> 19% of each run, Pallas kernels for 4% -> 8%
where the time goes in v3:
time: 210 us; the launch traced here: 209 us
  waiting for transfers between devices  119 us (57%)
  starting transfers between devices  29.8 us (14%)
  local copies, waits for them, and re-layouts  25.6 us (12%)
  other arithmetic  17.6 us (8%)
  Pallas kernels  16.3 us (8%)
    all_to_all x1, waiting for transfers between devices, local(): lax.all_to_all(applied_sent, 'region', split_axis=1, concat_axis=0, tiled...  36.5 us
    all_to_all x1, waiting for transfers between devices, local(): lax.all_to_all(sent, 'region', split_axis=1, concat_axis=0, tiled=True)  36 us
    ppermute x4, waiting for transfers between devices, halved(): lax.ppermute(given, 'pair', [(i, i ^ bit) for i in range(count)])  25.2 us
    pallas_call x2, Pallas kernels, pair_blocks(): pl.pallas_call(pair_kernel, out_shape=jax.ShapeDtypeStruct((count, W, W),...  16.3 us
    unnamed x22, local copies, waits for them, and re-layouts  10.7 us
    ppermute x1, waiting for transfers between devices, local(): low = lax.ppermute(confined[:, :, -1:], 'pair', forward)  10.6 us
    all_to_all x2, starting transfers between devices, reduced(): lax.all_to_all(sums, 'region', split_axis=0, concat_axis=0, tiled=True)  9.26 us
    all_to_all x2, waiting for transfers between devices, reduced(): lax.all_to_all(sums, 'region', split_axis=0, concat_axis=0, tiled=True)  8.79 us
  transfers between devices with their start and end apart: 13, of which 8 were waited for; matrix products, arithmetic and copies ran while one was open for 19% of the time, Pallas kernels for 8%

profile of v3, /device:TPU:0, one launch (start us, length us, event | category | flops | bytes accessed | tf_op | source)
XLA Modules:
  0.0 209.3 jit_solution(11081217746109415251)
XLA Ops:
  0.6 3.0 %collective-permute-start.2 = (f32[1,8,128]{2,1,0:T(8,128)}, f32[1,8,128]{2,1,0:T(8,128)S(1)}, u32[]{:S(2)}, u32[]{:S(2)}) collective-permute-start(f32[1,8,128]{2,1,0:T(8,128)} %param.5), channel_id=1, source_target_pairs={{0,4},{4,0},{8,12},{12,8},{16,20},{20,16},{24,28},{28,24},{1,5},{5... | collective-permute-start | bytes 12296 | tf_op jit(solution)/shard_map/ppermute | solution.py:49
  6.1 2.1 %collective-permute-start.3 = (f32[2,8,128]{2,1,0:T(8,128)S(1)}, f32[2,8,128]{2,1,0:T(8,128)S(1)}, u32[]{:S(2)}, u32[]{:S(2)}) collective-permute-start(f32[2,8,128]{2,1,0:T(8,128)S(1)} %pad_maximum_fusion.2), channel_id=1, source_target_pairs={{0,8},{4,12},{8,0},{12,4},{16,24},{20,28},{24,16},{28,20},{1,9},{5... | collective-permute-start | bytes 24584 | tf_op jit(solution)/shard_map/ppermute | solution.py:49
  8.2 6.5 %fusion.10 = (f32[128,8,8,128]{3,2,0,1:T(8,128)}, bf16[128,8,8,128]{3,2,0,1:T(8,128)(2,1)}) fusion(bf16[128,8,8,128]{3,2,1,0:T(8,128)(2,1)} %param.4, pred[128,8]{0,1:T(8,128)(4,1)S(1)} %broadcast_compare_fusion), kind=kLoop, calls=%fused_computation.43 | loop fusion | flops 2097152 | bytes 8389632 | tf_op jit(solution)/shard_map/convert_element_type | solution.py:101
  14.8 2.7 %collective-permute-start.4 = (f32[4,8,128]{2,1,0:T(8,128)S(1)}, f32[4,8,128]{2,1,0:T(8,128)S(1)}, u32[]{:S(2)}, u32[]{:S(2)}) collective-permute-start(f32[4,8,128]{2,1,0:T(8,128)S(1)} %pad_maximum_fusion.1), channel_id=1, source_target_pairs={{0,16},{4,20},{8,24},{12,28},{16,0},{20,4},{24,8},{28,12},{1,17},{... | collective-permute-start | bytes 49160 | tf_op jit(solution)/shard_map/ppermute | solution.py:49
  17.4 3.3 %fusion.14 = (bf16[128,8,1,128]{3,2,0,1:T(2,128)(2,1)S(1)}, bf16[128,8,1,128]{3,2,0,1:T(2,128)(2,1)S(1)}) fusion(bf16[128,8,8,128]{3,2,0,1:T(8,128)(2,1)} %get-tuple-element.9), kind=kLoop, calls=%fused_computation.47 | loop fusion | bytes 1048576 | tf_op jit(solution)/shard_map/slice | solution.py:94
  20.8 1.7 collective-permute-start.1
  22.5 10.6 %collective-permute-done = bf16[128,8,1,128]{3,2,0,1:T(2,128)(2,1)S(1)} collective-permute-done((bf16[128,8,1,128]{3,2,0,1:T(2,128)(2,1)S(1)}, bf16[128,8,1,128]{3,2,0,1:T(2,128)(2,1)S(1)}, u32[]{:S(2)}, u32[]{:S(2)}) %collective-permute-start) | collective-permute-done | bytes 262176 | tf_op jit(solution)/shard_map/ppermute | solution.py:93
  34.0 3.6 %all-to-all-start = ((bf16[128,8,8,128]{3,2,0,1:T(8,128)(2,1)}), bf16[128,8,8,128]{3,2,0,1:T(8,128)(2,1)S(1)}, u32[]{:S(2)}, u32[]{:S(2)}) async-start(bf16[128,8,8,128]{3,2,0,1:T(8,128)(2,1)} %get-tuple-element.9), calls=%async_computation | async-start | bytes 4194304 | tf_op jit(solution)/shard_map/all_to_all | solution.py:99
  37.7 1.1 fusion.12
  38.8 2.8 %fusion.13 = (f32[128,7,8,128]{3,2,0,1:T(8,128)S(1)}, f32[128,7,8,128]{3,2,0,1:T(8,128)S(1)}) fusion(bf16[128,8,8,128]{3,2,0,1:T(8,128)(2,1)} %get-tuple-element.9), kind=kLoop, calls=%fused_computation.46 | loop fusion | bytes 14680064 | tf_op jit(solution)/shard_map/jit(_roll_static)/slice | solution.py:102
  41.6 3.2 %fusion.11 = (f32[128,8,7,128]{3,2,0,1:T(8,128)S(1)}, f32[128,8,7,128]{3,2,0,1:T(8,128)S(1)}) fusion(bf16[128,8,8,128]{3,2,0,1:T(8,128)(2,1)} %get-tuple-element.9), kind=kLoop, calls=%fused_computation.44 | loop fusion | bytes 14680064 | tf_op jit(solution)/shard_map/slice | solution.py:103
  45.9 5.2 %fusion.5 = bf16[128,8,8,128]{3,2,0,1:T(8,128)(2,1)} fusion(f32[128,8,8,128]{3,2,0,1:T(8,128)S(1)} %copy-done.5, f32[128,1,8,128]{3,2,0,1:T(8,128)S(1)} %get-tuple-element.32, f32[128,7,8,128]{3,2,0,1:T(8,128)S(1)} %get-tuple-element.34, f32[128,7,8,128]{3,2,0,1:T(8,128)S(1)} %get-tuple-element.33, f32[128,1,8,128]{3,2,0,1:T(8,128)S(1)} %get-tuple-element.31, ...), kind=kLoop, calls=%fused_computation.8 | loop fusion | flops 16777216 | bytes 23105536 | tf_op jit(solution)/shard_map/convert_element_type | solution.py:109
  51.1 36.0 %all-to-all-done = bf16[128,8,8,128]{3,2,0,1:T(8,128)(2,1)S(1)} async-done(((bf16[128,8,8,128]{3,2,0,1:T(8,128)(2,1)}), bf16[128,8,8,128]{3,2,0,1:T(8,128)(2,1)S(1)}, u32[]{:S(2)}, u32[]{:S(2)}) %all-to-all-start) | async-done | bytes 2097184 | tf_op jit(solution)/shard_map/all_to_all | solution.py:99
  87.1 4.3 %all-to-all-start.2 = ((bf16[128,8,8,128]{3,2,0,1:T(8,128)(2,1)}), bf16[128,8,8,128]{3,2,0,1:T(8,128)(2,1)}, u32[]{:S(2)}, u32[]{:S(2)}) async-start(bf16[128,8,8,128]{3,2,0,1:T(8,128)(2,1)} %fusion.5), calls=%async_computation.2 | async-start | bytes 4194304 | tf_op jit(solution)/shard_map/all_to_all | solution.py:111
  91.6 2.2 %copy.57 = bf16[128,8,8,128]{3,1,2,0:T(8,128)(2,1)S(1)} copy(bf16[128,8,8,128]{3,2,1,0:T(8,128)(2,1)} %bitcast.54) | data formatting | bytes 4194304
  93.8 8.2 %shard_map.67 = f32[32,128,128]{2,1,0:T(8,128)S(1)} custom-call(s32[32,2]{1,0:T(8,128)S(1)} %copy.37.pairs_ref, bf16[1024,1024]{1,0:T(8,128)(2,1)S(1)} %bitcast.46, bf16[1024,1024]{1,0:T(8,128)(2,1)S(1)} %bitcast.47), custom_call_target="tpu_custom_call" | custom-call | flops 1073741824 | bytes 6291456 | tf_op jit(solution)/shard_map/pallas_call | solution.py:26
  102.0 1.3 copy-done.1
  103.6 36.5 %all-to-all-done.2 = bf16[128,8,8,128]{3,2,0,1:T(8,128)(2,1)} async-done(((bf16[128,8,8,128]{3,2,0,1:T(8,128)(2,1)}), bf16[128,8,8,128]{3,2,0,1:T(8,128)(2,1)}, u32[]{:S(2)}, u32[]{:S(2)}) %all-to-all-start.2) | async-done | bytes 2097184 | tf_op jit(solution)/shard_map/all_to_all | solution.py:111
  140.1 2.2 %copy.56 = bf16[128,8,8,128]{3,1,2,0:T(8,128)(2,1)S(1)} copy(bf16[128,8,8,128]{3,2,1,0:T(8,128)(2,1)} %bitcast.29) | data formatting | bytes 4194304
  142.3 8.1 %shard_map.68 = f32[32,128,128]{2,1,0:T(8,128)S(1)} custom-call(s32[32,2]{1,0:T(8,128)S(1)} %copy.37.pairs_ref, bf16[1024,1024]{1,0:T(8,128)(2,1)S(1)} %bitcast.48, bf16[1024,1024]{1,0:T(8,128)(2,1)S(1)} %bitcast.53), custom_call_target="tpu_custom_call" | custom-call | flops 1073741824 | bytes 6291456 | tf_op jit(solution)/shard_map/pallas_call | solution.py:26
  150.4 1.2 dynamic-slice_bitcast_fusion
  151.6 1.4 bitcast_add_fusion.1
  153.8 1.4 collective-permute-start.6
  155.3 13.2 %collective-permute-done.6 = f32[1,8,128,128]{3,2,1,0:T(8,128)} collective-permute-done((f32[1,8,128,128]{3,2,1,0:T(8,128)}, f32[1,8,128,128]{3,2,1,0:T(8,128)}, u32[]{:S(2)}, u32[]{:S(2)}) %collective-permute-start.6) | collective-permute-done | bytes 524320 | tf_op jit(solution)/shard_map/ppermute | solution.py:63
  168.5 1.1 dynamic-slice_add_fusion.1
  170.5 3.6 %all-to-all-start.1 = ((f32[8,8,16,128]{3,2,1,0:T(8,128)}), f32[8,8,16,128]{3,2,1,0:T(8,128)S(1)}, u32[]{:S(2)}, u32[]{:S(2)}) async-start(f32[8,8,16,128]{3,2,1,0:T(8,128)} %copy.38), calls=%async_computation.1 | async-start | bytes 1048576 | tf_op jit(solution)/shard_map/all_to_all | solution.py:79
  174.1 1.4 bitcast_add_fusion
  175.6 1.5 collective-permute-start.8
  177.1 12.0 %collective-permute-done.8 = f32[1,8,128,128]{3,2,1,0:T(8,128)S(1)} collective-permute-done((f32[1,8,128,128]{3,2,1,0:T(8,128)S(1)}, f32[1,8,128,128]{3,2,1,0:T(8,128)S(1)}, u32[]{:S(2)}, u32[]{:S(2)}) %collective-permute-start.8) | collective-permute-done | bytes 524320 | tf_op jit(solution)/shard_map/ppermute | solution.py:63
  190.0 5.6 %all-to-all-start.3 = ((f32[8,8,16,128]{3,2,1,0:T(8,128)}), f32[8,8,16,128]{3,2,1,0:T(8,128)S(1)}, u32[]{:S(2)}, u32[]{:S(2)}) async-start(f32[8,8,16,128]{3,2,1,0:T(8,128)} %copy.41), calls=%async_computation.3 | async-start | bytes 1048576 | tf_op jit(solution)/shard_map/all_to_all | solution.py:79
  195.6 3.5 %copy.43 = bf16[128,8,8,128]{3,2,1,0:T(8,128)(2,1)} copy(bf16[128,8,8,128]{3,2,0,1:T(8,128)(2,1)} %fusion.5) | data formatting | bytes 4194304
  199.8 8.8 %all-to-all-done.3 = f32[8,8,16,128]{3,2,1,0:T(8,128)S(1)} async-done(((f32[8,8,16,128]{3,2,1,0:T(8,128)}), f32[8,8,16,128]{3,2,1,0:T(8,128)S(1)}, u32[]{:S(2)}, u32[]{:S(2)}) %all-to-all-start.3) | async-done | bytes 524320 | tf_op jit(solution)/shard_map/all_to_all | solution.py:79
  (50 shorter events, 8.9 us)
Async XLA Ops:
  0.6 3.0 %copy-start = (s32[8,8]{1,0:T(8,128)S(1)}, s32[8,8]{1,0:T(8,128)}, u32[]{:S(2)}) copy-start(s32[8,8]{1,0:T(8,128)} %param.7) | copy-start | bytes 772
  0.6 4.8 %collective-permute-start.2 = (f32[1,8,128]{2,1,0:T(8,128)}, f32[1,8,128]{2,1,0:T(8,128)S(1)}, u32[]{:S(2)}, u32[]{:S(2)}) collective-permute-start(f32[1,8,128]{2,1,0:T(8,128)} %param.5), channel_id=1, source_target_pairs={{0,4},{4,0},{8,12},{12,8},{16,20},{20,16},{24,28},{28,24},{1,5},{5... | collective-permute-start | bytes 12296 | tf_op jit(solution)/shard_map/ppermute | solution.py:49
  6.1 8.6 %collective-permute-start.3 = (f32[2,8,128]{2,1,0:T(8,128)S(1)}, f32[2,8,128]{2,1,0:T(8,128)S(1)}, u32[]{:S(2)}, u32[]{:S(2)}) collective-permute-start(f32[2,8,128]{2,1,0:T(8,128)S(1)} %pad_maximum_fusion.2), channel_id=1, source_target_pairs={{0,8},{4,12},{8,0},{12,4},{16,24},{20,28},{24,16},{28,20},{1,9},{5... | collective-permute-start | bytes 24584 | tf_op jit(solution)/shard_map/ppermute | solution.py:49
  14.8 7.7 %collective-permute-start.4 = (f32[4,8,128]{2,1,0:T(8,128)S(1)}, f32[4,8,128]{2,1,0:T(8,128)S(1)}, u32[]{:S(2)}, u32[]{:S(2)}) collective-permute-start(f32[4,8,128]{2,1,0:T(8,128)S(1)} %pad_maximum_fusion.1), channel_id=1, source_target_pairs={{0,16},{4,20},{8,24},{12,28},{16,0},{20,4},{24,8},{28,12},{1,17},{... | collective-permute-start | bytes 49160 | tf_op jit(solution)/shard_map/ppermute | solution.py:49
  20.7 12.4 %collective-permute-start = (bf16[128,8,1,128]{3,2,0,1:T(2,128)(2,1)S(1)}, bf16[128,8,1,128]{3,2,0,1:T(2,128)(2,1)S(1)}, u32[]{:S(2)}, u32[]{:S(2)}) collective-permute-start(bf16[128,8,1,128]{3,2,0,1:T(2,128)(2,1)S(1)} %get-tuple-element.36), channel_id=1, source_target_pairs={{0,1},{1,2},{2,3},{3,0},{4,5},{5,6},{6,7},{7,4},{8,9},{9,10},{10,1... | collective-permute-start | bytes 786440 | tf_op jit(solution)/shard_map/ppermute | solution.py:93
  20.8 13.2 %collective-permute-start.1 = (bf16[128,8,1,128]{3,2,0,1:T(2,128)(2,1)S(1)}, bf16[128,8,1,128]{3,2,0,1:T(2,128)(2,1)S(1)}, u32[]{:S(2)}, u32[]{:S(2)}) collective-permute-start(bf16[128,8,1,128]{3,2,0,1:T(2,128)(2,1)S(1)} %get-tuple-element.35), channel_id=1, source_target_pairs={{1,0},{2,1},{3,2},{0,3},{5,4},{6,5},{7,6},{4,7},{9,8},{10,9},{11,1... | collective-permute-start | bytes 786440 | tf_op jit(solution)/shard_map/ppermute | solution.py:94
  34.0 53.1 %all-to-all-start = ((bf16[128,8,8,128]{3,2,0,1:T(8,128)(2,1)}), bf16[128,8,8,128]{3,2,0,1:T(8,128)(2,1)S(1)}, u32[]{:S(2)}, u32[]{:S(2)}) async-start(bf16[128,8,8,128]{3,2,0,1:T(8,128)(2,1)} %get-tuple-element.9), calls=%async_computation | async-start | bytes 4194304 | tf_op jit(solution)/shard_map/all_to_all | solution.py:99
  41.6 4.3 %copy-start.5 = (f32[128,8,8,128]{3,2,0,1:T(8,128)S(1)}, f32[128,8,8,128]{3,2,0,1:T(8,128)}, u32[]{:S(2)}) copy-start(f32[128,8,8,128]{3,2,0,1:T(8,128)} %get-tuple-element.27) | copy-start | bytes 12582916
  51.1 40.4 %copy-start.7 = (s32[32,2]{0,1:T(2,128)S(1)}, s32[32,2]{0,1:T(2,128)}, u32[]{:S(2)}) copy-start(s32[32,2]{0,1:T(2,128)} %param.6) | copy-start | bytes 772
  87.1 4.5 %copy-start.6 = (bf16[128,8,8,128]{3,2,0,1:T(8,128)(2,1)}, bf16[128,8,8,128]{3,2,0,1:T(8,128)(2,1)S(1)}, u32[]{:S(2)}) copy-start(bf16[128,8,8,128]{3,2,0,1:T(8,128)(2,1)S(1)} %all-to-all-done) | copy-start | bytes 6291460
  87.1 52.9 %all-to-all-start.2 = ((bf16[128,8,8,128]{3,2,0,1:T(8,128)(2,1)}), bf16[128,8,8,128]{3,2,0,1:T(8,128)(2,1)}, u32[]{:S(2)}, u32[]{:S(2)}) async-start(bf16[128,8,8,128]{3,2,0,1:T(8,128)(2,1)} %fusion.5), calls=%async_computation.2 | async-start | bytes 4194304 | tf_op jit(solution)/shard_map/all_to_all | solution.py:111
  102.0 1.3 copy-start.1
  103.5 48.1 %collective-permute-start.5 = (f32[2,8,128,128]{3,2,1,0:T(8,128)S(1)}, f32[2,8,128,128]{3,2,1,0:T(8,128)}, u32[]{:S(2)}, u32[]{:S(2)}) collective-permute-start(f32[2,8,128,128]{3,2,1,0:T(8,128)S(1)} %dynamic-slice_bitcast_fusion.1), channel_id=1, source_target_pairs={{0,1},{1,0},{2,3},{3,2},{4,5},{5,4},{6,7},{7,6},{8,9},{9,8},{10,11... | collective-permute-start | bytes 3145736 | tf_op jit(solution)/shard_map/ppermute | solution.py:63
  142.3 9.3 %copy-start.2 = (f32[32,128,128]{2,1,0:T(8,128)S(1)}, f32[32,128,128]{2,1,0:T(8,128)}, u32[]{:S(2)}) copy-start(f32[32,128,128]{2,1,0:T(8,128)} %copy-done.1) | copy-start | bytes 6291460
  150.4 2.6 %copy-start.3 = (f32[32,128,128]{2,1,0:T(8,128)}, f32[32,128,128]{2,1,0:T(8,128)S(1)}, u32[]{:S(2)}) copy-start(f32[32,128,128]{2,1,0:T(8,128)S(1)} %shard_map.68) | copy-start | bytes 6291460
  151.6 22.5 %collective-permute-start.7 = (f32[2,8,128,128]{3,2,1,0:T(8,128)}, f32[2,8,128,128]{3,2,1,0:T(8,128)}, u32[]{:S(2)}, u32[]{:S(2)}) collective-permute-start(f32[2,8,128,128]{3,2,1,0:T(8,128)} %dynamic-slice_bitcast_fusion), channel_id=1, source_target_pairs={{0,1},{1,0},{2,3},{3,2},{4,5},{5,4},{6,7},{7,6},{8,9},{9,8},{10,11... | collective-permute-start | bytes 3145736 | tf_op jit(solution)/shard_map/ppermute | solution.py:63
  153.8 20.2 %copy-start.4 = (f32[32,128,128]{2,1,0:T(8,128)S(1)}, f32[32,128,128]{2,1,0:T(8,128)}, u32[]{:S(2)}) copy-start(f32[32,128,128]{2,1,0:T(8,128)} %copy-done.3) | copy-start | bytes 6291460
  153.8 14.6 %collective-permute-start.6 = (f32[1,8,128,128]{3,2,1,0:T(8,128)}, f32[1,8,128,128]{3,2,1,0:T(8,128)}, u32[]{:S(2)}, u32[]{:S(2)}) collective-permute-start(f32[1,8,128,128]{3,2,1,0:T(8,128)} %constant_dynamic-slice_fusion.1), channel_id=1, source_target_pairs={{0,2},{1,3},{2,0},{3,1},{4,6},{5,7},{6,4},{7,5},{8,10},{9,11},{10,... | collective-permute-start | bytes 1572872 | tf_op jit(solution)/shard_map/ppermute | solution.py:63
  170.5 19.5 %all-to-all-start.1 = ((f32[8,8,16,128]{3,2,1,0:T(8,128)}), f32[8,8,16,128]{3,2,1,0:T(8,128)S(1)}, u32[]{:S(2)}, u32[]{:S(2)}) async-start(f32[8,8,16,128]{3,2,1,0:T(8,128)} %copy.38), calls=%async_computation.1 | async-start | bytes 1048576 | tf_op jit(solution)/shard_map/all_to_all | solution.py:79
  175.6 13.5 %collective-permute-start.8 = (f32[1,8,128,128]{3,2,1,0:T(8,128)S(1)}, f32[1,8,128,128]{3,2,1,0:T(8,128)S(1)}, u32[]{:S(2)}, u32[]{:S(2)}) collective-permute-start(f32[1,8,128,128]{3,2,1,0:T(8,128)S(1)} %constant_dynamic-slice_fusion), channel_id=1, source_target_pairs={{0,2},{1,3},{2,0},{3,1},{4,6},{5,7},{6,4},{7,5},{8,10},{9,11},{10,... | collective-permute-start | bytes 1572872 | tf_op jit(solution)/shard_map/ppermute | solution.py:63
  190.0 18.6 %all-to-all-start.3 = ((f32[8,8,16,128]{3,2,1,0:T(8,128)}), f32[8,8,16,128]{3,2,1,0:T(8,128)S(1)}, u32[]{:S(2)}, u32[]{:S(2)}) async-start(f32[8,8,16,128]{3,2,1,0:T(8,128)} %copy.41), calls=%async_computation.3 | async-start | bytes 1048576 | tf_op jit(solution)/shard_map/all_to_all | solution.py:79

commit v4 on v3

--- a/solution.py
+++ b/solution.py
@@ -63,9 +63,8 @@
     return kept + lax.ppermute(given, "pair", [(i, i ^ bit) for i in range(count)])
 
 
-def reduced(blocks):
+def pair_reduced(blocks):
     count = lax.axis_size("pair")
-    region_count = lax.axis_size("region")
     listed = blocks.shape[0] // count
     parts = blocks.reshape(count, listed, W, W)
     bit = 1
@@ -74,6 +73,12 @@
         parts = parts.reshape(rest, 2, listed, W, W).swapaxes(0, 1)
         parts = halved(parts, bit)
         bit *= 2
+    return parts
+
+
+def region_reduced(parts):
+    region_count = lax.axis_size("region")
+    listed = parts.size // (W * W)
     width = W // region_count
     sums = parts.reshape(listed, region_count, width, W).swapaxes(0, 1)
     sums = lax.all_to_all(sums, "region", split_axis=0, concat_axis=0, tiled=True)
@@ -113,8 +118,10 @@
     flat = (func_count * region_count, -1)
     data = data.reshape(flat)
     applied_data = applied_data.reshape(flat)
-    intersection = reduced(pair_blocks(pair_list, data, data))
-    hamiltonian = reduced(pair_blocks(pair_list, data, applied_data))
+    shares = pair_reduced(pair_blocks(pair_list, data, data))
+    shares, applied_data = lax.optimization_barrier((shares, applied_data))
+    intersection = region_reduced(shares)
+    hamiltonian = region_reduced(pair_reduced(pair_blocks(pair_list, data, applied_data)))
     return intersection, hamiltonian, applied
 
 

time: 210 us -> 194 us (0.924)
  waiting for transfers between devices: 119 us -> 102 us
    all_to_all x1, waiting for transfers between devices: 36.5 us -> 15 us  [local(): lax.all_to_all(applied_sent, 'region', split_axis=1, concat_axis=0, tiled...]
    ppermute x4, waiting for transfers between devices: 25.2 us -> 28.5 us  [halved(): lax.ppermute(given, 'pair', [(i, i ^ bit) for i in range(count)])]
    unnamed x22 -> x20, local copies, waits for them, and re-layouts: 10.7 us -> 12 us
  transfers between devices with their start and end apart: 13 -> 13, of which waited for: 8 -> 9; matrix products, arithmetic and copies ran while one was open for 19% -> 20% of each run, Pallas kernels for 8% -> 4%
where the time goes in v4:
time: 194 us; the launch traced here: 193 us
  waiting for transfers between devices  102 us (53%)
  starting transfers between devices  29.7 us (15%)
  local copies, waits for them, and re-layouts  25.7 us (13%)
  other arithmetic  18.7 us (10%)
  Pallas kernels  16.4 us (8%)
    all_to_all x1, waiting for transfers between devices, local(): lax.all_to_all(sent, 'region', split_axis=1, concat_axis=0, tiled=True)  36.1 us
    ppermute x4, waiting for transfers between devices, halved(): lax.ppermute(given, 'pair', [(i, i ^ bit) for i in range(count)])  28.5 us
    pallas_call x2, Pallas kernels, pair_blocks(): pl.pallas_call(pair_kernel, out_shape=jax.ShapeDtypeStruct((count, W, W),...  16.4 us
    all_to_all x1, waiting for transfers between devices, local(): lax.all_to_all(applied_sent, 'region', split_axis=1, concat_axis=0, tiled...  15 us
    unnamed x20, local copies, waits for them, and re-layouts  12 us
    ppermute x1, waiting for transfers between devices, local(): low = lax.ppermute(confined[:, :, -1:], 'pair', forward)  10.6 us
    all_to_all x2, waiting for transfers between devices, region_reduced(): lax.all_to_all(sums, 'region', split_axis=0, concat_axis=0, tiled=True)  9.69 us
    all_to_all x2, starting transfers between devices, region_reduced(): lax.all_to_all(sums, 'region', split_axis=0, concat_axis=0, tiled=True)  9.25 us
  transfers between devices with their start and end apart: 13, of which 9 were waited for; matrix products, arithmetic and copies ran while one was open for 20% of the time, Pallas kernels for 4%

profile of v4, /device:TPU:0, one launch (start us, length us, event | category | flops | bytes accessed | tf_op | source)
XLA Modules:
  0.0 193.4 jit_solution(5358044759171652145)
XLA Ops:
  0.6 3.0 %collective-permute-start.2 = (f32[1,8,128]{2,1,0:T(8,128)}, f32[1,8,128]{2,1,0:T(8,128)S(1)}, u32[]{:S(2)}, u32[]{:S(2)}) collective-permute-start(f32[1,8,128]{2,1,0:T(8,128)} %param.5), channel_id=1, source_target_pairs={{0,4},{4,0},{8,12},{12,8},{16,20},{20,16},{24,28},{28,24},{1,5},{5... | collective-permute-start | bytes 12296 | tf_op jit(solution)/shard_map/ppermute | solution.py:49
  6.1 2.1 %collective-permute-start.3 = (f32[2,8,128]{2,1,0:T(8,128)S(1)}, f32[2,8,128]{2,1,0:T(8,128)S(1)}, u32[]{:S(2)}, u32[]{:S(2)}) collective-permute-start(f32[2,8,128]{2,1,0:T(8,128)S(1)} %pad_maximum_fusion.2), channel_id=1, source_target_pairs={{0,8},{4,12},{8,0},{12,4},{16,24},{20,28},{24,16},{28,20},{1,9},{5... | collective-permute-start | bytes 24584 | tf_op jit(solution)/shard_map/ppermute | solution.py:49
  8.2 6.5 %fusion.10 = (f32[128,8,8,128]{3,2,0,1:T(8,128)}, bf16[128,8,8,128]{3,2,0,1:T(8,128)(2,1)}) fusion(bf16[128,8,8,128]{3,2,1,0:T(8,128)(2,1)} %param.4, pred[128,8]{0,1:T(8,128)(4,1)S(1)} %broadcast_compare_fusion), kind=kLoop, calls=%fused_computation.43 | loop fusion | flops 2097152 | bytes 8389632 | tf_op jit(solution)/shard_map/convert_element_type | solution.py:106
  14.8 2.7 %collective-permute-start.4 = (f32[4,8,128]{2,1,0:T(8,128)S(1)}, f32[4,8,128]{2,1,0:T(8,128)S(1)}, u32[]{:S(2)}, u32[]{:S(2)}) collective-permute-start(f32[4,8,128]{2,1,0:T(8,128)S(1)} %pad_maximum_fusion.1), channel_id=1, source_target_pairs={{0,16},{4,20},{8,24},{12,28},{16,0},{20,4},{24,8},{28,12},{1,17},{... | collective-permute-start | bytes 49160 | tf_op jit(solution)/shard_map/ppermute | solution.py:49
  17.5 3.2 %fusion.14 = (bf16[128,8,1,128]{3,2,0,1:T(2,128)(2,1)S(1)}, bf16[128,8,1,128]{3,2,0,1:T(2,128)(2,1)S(1)}) fusion(bf16[128,8,8,128]{3,2,0,1:T(8,128)(2,1)} %get-tuple-element.11), kind=kLoop, calls=%fused_computation.47 | loop fusion | bytes 1048576 | tf_op jit(solution)/shard_map/slice | solution.py:99
  20.8 1.7 collective-permute-start.1
  22.5 10.6 %collective-permute-done = bf16[128,8,1,128]{3,2,0,1:T(2,128)(2,1)S(1)} collective-permute-done((bf16[128,8,1,128]{3,2,0,1:T(2,128)(2,1)S(1)}, bf16[128,8,1,128]{3,2,0,1:T(2,128)(2,1)S(1)}, u32[]{:S(2)}, u32[]{:S(2)}) %collective-permute-start) | collective-permute-done | bytes 262176 | tf_op jit(solution)/shard_map/ppermute | solution.py:98
  34.0 3.6 %all-to-all-start = ((bf16[128,8,8,128]{3,2,0,1:T(8,128)(2,1)}), bf16[128,8,8,128]{3,2,0,1:T(8,128)(2,1)S(1)}, u32[]{:S(2)}, u32[]{:S(2)}) async-start(bf16[128,8,8,128]{3,2,0,1:T(8,128)(2,1)} %get-tuple-element.11), calls=%async_computation | async-start | bytes 4194304 | tf_op jit(solution)/shard_map/all_to_all | solution.py:104
  38.8 2.8 %fusion.13 = (f32[128,7,8,128]{3,2,0,1:T(8,128)S(1)}, f32[128,7,8,128]{3,2,0,1:T(8,128)S(1)}) fusion(bf16[128,8,8,128]{3,2,0,1:T(8,128)(2,1)} %get-tuple-element.11), kind=kLoop, calls=%fused_computation.46 | loop fusion | bytes 14680064 | tf_op jit(solution)/shard_map/jit(_roll_static)/slice | solution.py:107
  41.5 3.2 %fusion.11 = (f32[128,8,7,128]{3,2,0,1:T(8,128)S(1)}, f32[128,8,7,128]{3,2,0,1:T(8,128)S(1)}) fusion(bf16[128,8,8,128]{3,2,0,1:T(8,128)(2,1)} %get-tuple-element.11), kind=kLoop, calls=%fused_computation.44 | loop fusion | bytes 14680064 | tf_op jit(solution)/shard_map/slice | solution.py:108
  45.9 5.2 %fusion.5 = bf16[128,8,8,128]{3,2,0,1:T(8,128)(2,1)} fusion(f32[128,8,8,128]{3,2,0,1:T(8,128)S(1)} %copy-done.3, f32[128,1,8,128]{3,2,0,1:T(8,128)S(1)} %get-tuple-element.36, f32[128,7,8,128]{3,2,0,1:T(8,128)S(1)} %get-tuple-element.38, f32[128,7,8,128]{3,2,0,1:T(8,128)S(1)} %get-tuple-element.37, f32[128,1,8,128]{3,2,0,1:T(8,128)S(1)} %get-tuple-element.35, ...), kind=kLoop, calls=%fused_computation.8 | loop fusion | flops 16777216 | bytes 23105536 | tf_op jit(solution)/shard_map/convert_element_type | solution.py:114
  51.0 36.1 %all-to-all-done = bf16[128,8,8,128]{3,2,0,1:T(8,128)(2,1)S(1)} async-done(((bf16[128,8,8,128]{3,2,0,1:T(8,128)(2,1)}), bf16[128,8,8,128]{3,2,0,1:T(8,128)(2,1)S(1)}, u32[]{:S(2)}, u32[]{:S(2)}) %all-to-all-start) | async-done | bytes 2097184 | tf_op jit(solution)/shard_map/all_to_all | solution.py:104
  87.1 4.4 %all-to-all-start.1 = ((bf16[128,8,8,128]{3,2,0,1:T(8,128)(2,1)}), bf16[128,8,8,128]{3,2,0,1:T(8,128)(2,1)}, u32[]{:S(2)}, u32[]{:S(2)}) async-start(bf16[128,8,8,128]{3,2,0,1:T(8,128)(2,1)} %fusion.5), calls=%async_computation.1 | async-start | bytes 4194304 | tf_op jit(solution)/shard_map/all_to_all | solution.py:116
  91.6 2.2 %copy.57 = bf16[128,8,8,128]{3,1,2,0:T(8,128)(2,1)S(1)} copy(bf16[128,8,8,128]{3,2,1,0:T(8,128)(2,1)} %bitcast.54) | data formatting | bytes 4194304
  93.8 8.2 %shard_map.67 = f32[32,128,128]{2,1,0:T(8,128)S(1)} custom-call(s32[32,2]{1,0:T(8,128)S(1)} %copy.37.pairs_ref, bf16[1024,1024]{1,0:T(8,128)(2,1)S(1)} %bitcast.46, bf16[1024,1024]{1,0:T(8,128)(2,1)S(1)} %bitcast.47), custom_call_target="tpu_custom_call" | custom-call | flops 1073741824 | bytes 6291456 | tf_op jit(solution)/shard_map/pallas_call | solution.py:26
  102.1 1.3 copy-done.1
  103.6 2.7 %collective-permute-done.5 = f32[2,8,128,128]{3,2,1,0:T(8,128)} collective-permute-done((f32[2,8,128,128]{3,2,1,0:T(8,128)S(1)}, f32[2,8,128,128]{3,2,1,0:T(8,128)}, u32[]{:S(2)}, u32[]{:S(2)}) %collective-permute-start.5) | collective-permute-done | bytes 1048608 | tf_op jit(solution)/shard_map/ppermute | solution.py:63
  106.3 1.7 bitcast_add_fusion.1
  108.8 1.4 collective-permute-start.6
  110.3 12.9 %collective-permute-done.6 = f32[1,8,128,128]{3,2,1,0:T(8,128)} collective-permute-done((f32[1,8,128,128]{3,2,1,0:T(8,128)}, f32[1,8,128,128]{3,2,1,0:T(8,128)}, u32[]{:S(2)}, u32[]{:S(2)}) %collective-permute-start.6) | collective-permute-done | bytes 524320 | tf_op jit(solution)/shard_map/ppermute | solution.py:63
  123.1 1.9 %dynamic-slice_add_fusion.1 = f32[1,8,128,128]{3,2,1,0:T(8,128)} fusion(f32[1,8,128,128]{3,2,1,0:T(8,128)} %collective-permute-done.6, f32[2,8,128,128]{3,2,1,0:T(8,128)S(1)} %bitcast_add_fusion.1, s32[]{:T(128)S(6)} %select_n.143), kind=kLoop, calls=%fused_computation.21 | loop fusion | flops 131072 | bytes 1572868 | tf_op jit(solution)/shard_map/add | solution.py:63
  125.1 15.0 %all-to-all-done.1 = bf16[128,8,8,128]{3,2,0,1:T(8,128)(2,1)} async-done(((bf16[128,8,8,128]{3,2,0,1:T(8,128)(2,1)}), bf16[128,8,8,128]{3,2,0,1:T(8,128)(2,1)}, u32[]{:S(2)}, u32[]{:S(2)}) %all-to-all-start.1) | async-done | bytes 2097184 | tf_op jit(solution)/shard_map/all_to_all | solution.py:116
  140.1 2.2 %copy.56 = bf16[128,8,8,128]{3,1,2,0:T(8,128)(2,1)S(1)} copy(bf16[128,8,8,128]{3,2,1,0:T(8,128)(2,1)} %bitcast.27) | data formatting | bytes 4194304
  142.3 8.2 %shard_map.68 = f32[32,128,128]{2,1,0:T(8,128)S(1)} custom-call(s32[32,2]{1,0:T(8,128)S(1)} %copy.37.pairs_ref, bf16[1024,1024]{1,0:T(8,128)(2,1)S(1)} %bitcast.48, bf16[1024,1024]{1,0:T(8,128)(2,1)S(1)} %bitcast.53), custom_call_target="tpu_custom_call" | custom-call | flops 1073741824 | bytes 6291456 | tf_op jit(solution)/shard_map/pallas_call | solution.py:26
  150.6 1.3 copy-done.2
  152.9 3.6 %all-to-all-start.2 = ((f32[8,8,16,128]{3,2,1,0:T(8,128)}), f32[8,8,16,128]{3,2,1,0:T(8,128)S(1)}, u32[]{:S(2)}, u32[]{:S(2)}) async-start(f32[8,8,16,128]{3,2,1,0:T(8,128)} %copy.38), calls=%async_computation.2 | async-start | bytes 1048576 | tf_op jit(solution)/shard_map/all_to_all | solution.py:84
  156.5 1.4 bitcast_add_fusion
  158.0 1.4 collective-permute-start.8
  159.4 12.9 %collective-permute-done.8 = f32[1,8,128,128]{3,2,1,0:T(8,128)S(1)} collective-permute-done((f32[1,8,128,128]{3,2,1,0:T(8,128)S(1)}, f32[1,8,128,128]{3,2,1,0:T(8,128)S(1)}, u32[]{:S(2)}, u32[]{:S(2)}) %collective-permute-start.8) | collective-permute-done | bytes 524320 | tf_op jit(solution)/shard_map/ppermute | solution.py:63
  173.2 5.6 %all-to-all-start.3 = ((f32[8,8,16,128]{3,2,1,0:T(8,128)}), f32[8,8,16,128]{3,2,1,0:T(8,128)S(1)}, u32[]{:S(2)}, u32[]{:S(2)}) async-start(f32[8,8,16,128]{3,2,1,0:T(8,128)} %copy.41), calls=%async_computation.3 | async-start | bytes 1048576 | tf_op jit(solution)/shard_map/all_to_all | solution.py:84
  178.8 3.5 %copy.43 = bf16[128,8,8,128]{3,2,1,0:T(8,128)(2,1)} copy(bf16[128,8,8,128]{3,2,0,1:T(8,128)(2,1)} %fusion.5) | data formatting | bytes 4194304
  183.0 9.7 %all-to-all-done.3 = f32[8,8,16,128]{3,2,1,0:T(8,128)S(1)} async-done(((f32[8,8,16,128]{3,2,1,0:T(8,128)}), f32[8,8,16,128]{3,2,1,0:T(8,128)S(1)}, u32[]{:S(2)}, u32[]{:S(2)}) %all-to-all-start.3) | async-done | bytes 524320 | tf_op jit(solution)/shard_map/all_to_all | solution.py:84
  (48 shorter events, 10.1 us)
Async XLA Ops:
  0.6 3.0 %copy-start = (s32[8,8]{1,0:T(8,128)S(1)}, s32[8,8]{1,0:T(8,128)}, u32[]{:S(2)}) copy-start(s32[8,8]{1,0:T(8,128)} %param.7) | copy-start | bytes 772
  0.6 4.8 %collective-permute-start.2 = (f32[1,8,128]{2,1,0:T(8,128)}, f32[1,8,128]{2,1,0:T(8,128)S(1)}, u32[]{:S(2)}, u32[]{:S(2)}) collective-permute-start(f32[1,8,128]{2,1,0:T(8,128)} %param.5), channel_id=1, source_target_pairs={{0,4},{4,0},{8,12},{12,8},{16,20},{20,16},{24,28},{28,24},{1,5},{5... | collective-permute-start | bytes 12296 | tf_op jit(solution)/shard_map/ppermute | solution.py:49
  6.1 8.7 %collective-permute-start.3 = (f32[2,8,128]{2,1,0:T(8,128)S(1)}, f32[2,8,128]{2,1,0:T(8,128)S(1)}, u32[]{:S(2)}, u32[]{:S(2)}) collective-permute-start(f32[2,8,128]{2,1,0:T(8,128)S(1)} %pad_maximum_fusion.2), channel_id=1, source_target_pairs={{0,8},{4,12},{8,0},{12,4},{16,24},{20,28},{24,16},{28,20},{1,9},{5... | collective-permute-start | bytes 24584 | tf_op jit(solution)/shard_map/ppermute | solution.py:49
  14.8 7.7 %collective-permute-start.4 = (f32[4,8,128]{2,1,0:T(8,128)S(1)}, f32[4,8,128]{2,1,0:T(8,128)S(1)}, u32[]{:S(2)}, u32[]{:S(2)}) collective-permute-start(f32[4,8,128]{2,1,0:T(8,128)S(1)} %pad_maximum_fusion.1), channel_id=1, source_target_pairs={{0,16},{4,20},{8,24},{12,28},{16,0},{20,4},{24,8},{28,12},{1,17},{... | collective-permute-start | bytes 49160 | tf_op jit(solution)/shard_map/ppermute | solution.py:49
  20.7 12.4 %collective-permute-start = (bf16[128,8,1,128]{3,2,0,1:T(2,128)(2,1)S(1)}, bf16[128,8,1,128]{3,2,0,1:T(2,128)(2,1)S(1)}, u32[]{:S(2)}, u32[]{:S(2)}) collective-permute-start(bf16[128,8,1,128]{3,2,0,1:T(2,128)(2,1)S(1)} %get-tuple-element.40), channel_id=1, source_target_pairs={{0,1},{1,2},{2,3},{3,0},{4,5},{5,6},{6,7},{7,4},{8,9},{9,10},{10,1... | collective-permute-start | bytes 786440 | tf_op jit(solution)/shard_map/ppermute | solution.py:98
  20.8 13.2 %collective-permute-start.1 = (bf16[128,8,1,128]{3,2,0,1:T(2,128)(2,1)S(1)}, bf16[128,8,1,128]{3,2,0,1:T(2,128)(2,1)S(1)}, u32[]{:S(2)}, u32[]{:S(2)}) collective-permute-start(bf16[128,8,1,128]{3,2,0,1:T(2,128)(2,1)S(1)} %get-tuple-element.39), channel_id=1, source_target_pairs={{1,0},{2,1},{3,2},{0,3},{5,4},{6,5},{7,6},{4,7},{9,8},{10,9},{11,1... | collective-permute-start | bytes 786440 | tf_op jit(solution)/shard_map/ppermute | solution.py:99
  34.0 53.1 %all-to-all-start = ((bf16[128,8,8,128]{3,2,0,1:T(8,128)(2,1)}), bf16[128,8,8,128]{3,2,0,1:T(8,128)(2,1)S(1)}, u32[]{:S(2)}, u32[]{:S(2)}) async-start(bf16[128,8,8,128]{3,2,0,1:T(8,128)(2,1)} %get-tuple-element.11), calls=%async_computation | async-start | bytes 4194304 | tf_op jit(solution)/shard_map/all_to_all | solution.py:104
  41.5 4.3 %copy-start.3 = (f32[128,8,8,128]{3,2,0,1:T(8,128)S(1)}, f32[128,8,8,128]{3,2,0,1:T(8,128)}, u32[]{:S(2)}) copy-start(f32[128,8,8,128]{3,2,0,1:T(8,128)} %get-tuple-element.31) | copy-start | bytes 12582916
  51.0 40.5 %copy-start.6 = (s32[32,2]{0,1:T(2,128)S(1)}, s32[32,2]{0,1:T(2,128)}, u32[]{:S(2)}) copy-start(s32[32,2]{0,1:T(2,128)} %param.6) | copy-start | bytes 772
  87.1 4.5 %copy-start.4 = (bf16[128,8,8,128]{3,2,0,1:T(8,128)(2,1)}, bf16[128,8,8,128]{3,2,0,1:T(8,128)(2,1)S(1)}, u32[]{:S(2)}) copy-start(bf16[128,8,8,128]{3,2,0,1:T(8,128)(2,1)S(1)} %all-to-all-done) | copy-start | bytes 6291460
  87.1 53.0 %all-to-all-start.1 = ((bf16[128,8,8,128]{3,2,0,1:T(8,128)(2,1)}), bf16[128,8,8,128]{3,2,0,1:T(8,128)(2,1)}, u32[]{:S(2)}, u32[]{:S(2)}) async-start(bf16[128,8,8,128]{3,2,0,1:T(8,128)(2,1)} %fusion.5), calls=%async_computation.1 | async-start | bytes 4194304 | tf_op jit(solution)/shard_map/all_to_all | solution.py:116
  102.0 1.3 copy-start.1
  103.5 2.9 %collective-permute-start.5 = (f32[2,8,128,128]{3,2,1,0:T(8,128)S(1)}, f32[2,8,128,128]{3,2,1,0:T(8,128)}, u32[]{:S(2)}, u32[]{:S(2)}) collective-permute-start(f32[2,8,128,128]{3,2,1,0:T(8,128)S(1)} %dynamic-slice_bitcast_fusion.1), channel_id=1, source_target_pairs={{0,1},{1,0},{2,3},{3,2},{4,5},{5,4},{6,7},{7,6},{8,9},{9,8},{10,11... | collective-permute-start | bytes 3145736 | tf_op jit(solution)/shard_map/ppermute | solution.py:63
  108.8 14.3 %collective-permute-start.6 = (f32[1,8,128,128]{3,2,1,0:T(8,128)}, f32[1,8,128,128]{3,2,1,0:T(8,128)}, u32[]{:S(2)}, u32[]{:S(2)}) collective-permute-start(f32[1,8,128,128]{3,2,1,0:T(8,128)} %constant_dynamic-slice_fusion.1), channel_id=1, source_target_pairs={{0,2},{1,3},{2,0},{3,1},{4,6},{5,7},{6,4},{7,5},{8,10},{9,11},{10,... | collective-permute-start | bytes 1572872 | tf_op jit(solution)/shard_map/ppermute | solution.py:63
  142.3 9.7 %copy-start.5 = (f32[1,8,128,128]{3,2,1,0:T(8,128)S(1)}, f32[1,8,128,128]{3,2,1,0:T(8,128)}, u32[]{:S(2)}) copy-start(f32[1,8,128,128]{3,2,1,0:T(8,128)} %dynamic-slice_add_fusion.1) | copy-start | bytes 1572868
  150.5 1.3 copy-start.2
  151.9 4.6 %collective-permute-start.7 = (f32[2,8,128,128]{3,2,1,0:T(8,128)S(1)}, f32[2,8,128,128]{3,2,1,0:T(8,128)S(1)}, u32[]{:S(2)}, u32[]{:S(2)}) collective-permute-start(f32[2,8,128,128]{3,2,1,0:T(8,128)S(1)} %dynamic-slice_bitcast_fusion), channel_id=1, source_target_pairs={{0,1},{1,0},{2,3},{3,2},{4,5},{5,4},{6,7},{7,6},{8,9},{9,8},{10,11... | collective-permute-start | bytes 3145736 | tf_op jit(solution)/shard_map/ppermute | solution.py:63
  152.9 20.3 %all-to-all-start.2 = ((f32[8,8,16,128]{3,2,1,0:T(8,128)}), f32[8,8,16,128]{3,2,1,0:T(8,128)S(1)}, u32[]{:S(2)}, u32[]{:S(2)}) async-start(f32[8,8,16,128]{3,2,1,0:T(8,128)} %copy.38), calls=%async_computation.2 | async-start | bytes 1048576 | tf_op jit(solution)/shard_map/all_to_all | solution.py:84
  158.0 14.3 %collective-permute-start.8 = (f32[1,8,128,128]{3,2,1,0:T(8,128)S(1)}, f32[1,8,128,128]{3,2,1,0:T(8,128)S(1)}, u32[]{:S(2)}, u32[]{:S(2)}) collective-permute-start(f32[1,8,128,128]{3,2,1,0:T(8,128)S(1)} %constant_dynamic-slice_fusion), channel_id=1, source_target_pairs={{0,2},{1,3},{2,0},{3,1},{4,6},{5,7},{6,4},{7,5},{8,10},{9,11},{10,... | collective-permute-start | bytes 1572872 | tf_op jit(solution)/shard_map/ppermute | solution.py:63
  173.2 19.5 %all-to-all-start.3 = ((f32[8,8,16,128]{3,2,1,0:T(8,128)}), f32[8,8,16,128]{3,2,1,0:T(8,128)S(1)}, u32[]{:S(2)}, u32[]{:S(2)}) async-start(f32[8,8,16,128]{3,2,1,0:T(8,128)} %copy.41), calls=%async_computation.3 | async-start | bytes 1048576 | tf_op jit(solution)/shard_map/all_to_all | solution.py:84
